TPU v7x, 32 devices: a whole 2x2x4 slice. The times are simulated.
32 devices in a mesh: grp: 8 (over y, x, core), seq: 4 (over z).
Axes of the slice: x: 2, y: 2, z: 4, core: 2. Of those that a mesh axis runs over, the one named last changes fastest.
Arguments:
- lengths: int32 [16], replicated, may hold values from 42 to 1024, as said below
- group_of: int32 [16], replicated, may hold values from 0 to 7, as said below
- query_pre: bfloat16 [8192, 8192], P(('grp', 'seq')), may hold values from -170 to 170
- key_pre: bfloat16 [8192, 1024], P(('grp', 'seq')), may hold values from -7 to 7
- value_pre: bfloat16 [8192, 1024], P(('grp', 'seq')), may hold values from -4 to 4
- query_new: bfloat16 [16, 8192], P(None, 'seq'), may hold values from -170 to 170
- key_new: bfloat16 [16, 1024], P(None, 'seq'), may hold values from -4 to 4
- value_new: bfloat16 [16, 1024], P(None, 'seq'), may hold values from -4 to 4
- hidden_new: bfloat16 [16, 8192], P(None, 'grp'), may hold values from -3 to 3
- out_weight: bfloat16 [8192, 8192], P('seq', 'grp'), may hold values from -0.0625 to 0.0625
- norm_gain: bfloat16 [8192], P('grp'), may hold values from 0.099609375 to 1.8984375
- gate_weight: bfloat16 [8192, 16384], P('grp', 'seq'), may hold values from -0.0625 to 0.0625
- up_weight: bfloat16 [8192, 16384], P('grp', 'seq'), may hold values from -0.0625 to 0.0625
- down_weight: bfloat16 [16384, 8192], P('seq', 'grp'), may hold values from -0.046875 to 0.046875
Outputs:
- prefill_attention: bfloat16 [8192, 8192], P(('grp', 'seq'))
- decode_hidden: bfloat16 [16, 8192], P(None, ('grp', 'seq'))
Inputs may be any that keep to these rules, and one draw needn't show every extreme that they name: Two requests have length exactly 1024 and are alone in their groups; the others have lengths from 42 to 341; the lengths in one group sum to at most 1024. `group_of`: every group holds at least one request and at most three.
All inputs are finite; a program needn't handle non-finite values.
Results may differ from a plain program's by a relative error of at most 0.0095.
Values may be sent and summed in bfloat16 or wider, within the bound.
No kernel may reach another device: no remote copies, remote signals or barrier semaphores. Data moves between devices by JAX's collectives and lax.ppermute only.
A program may use at most 320 MiB of HBM per device.

v0:
```python
import math

import jax
import jax.numpy as jnp
from jax import lax
from jax.sharding import PartitionSpec as P

D = 8192
H = 64
KVH = 8
HD = 128


NEGATIVE = -1e30


def request_starts(lengths, group_of):
    index = jnp.arange(lengths.shape[0], dtype=jnp.int32)
    same = group_of[None, :] == group_of[:, None]
    before = index[None, :] < index[:, None]
    return jnp.sum(jnp.where(same & before, lengths[None, :], 0), axis=1)


def slot_owner(group_idx, starts, lengths, group_of, count):
    slots = jnp.arange(count, dtype=jnp.int32)
    inside = (
        (group_of[None, :] == group_idx)
        & (slots[:, None] >= starts[None, :])
        & (slots[:, None] < (starts + lengths)[None, :])
    )
    labels = jnp.arange(lengths.shape[0], dtype=jnp.int32) + 1
    return jnp.sum(jnp.where(inside, labels[None, :], 0), axis=1) - 1


def block_scores(queries, keys, owner_rows, owner_cols, row_first):
    count_q = queries.shape[0]
    count_k = keys.shape[0]
    kv_heads = keys.shape[1] // HD
    grouped = queries.shape[1] // (HD * kv_heads)
    query_heads = queries.reshape(count_q, kv_heads, grouped, HD)
    key_heads = keys.reshape(count_k, kv_heads, HD)
    scores = jnp.einsum(
        "qkgd,tkd->kgqt", query_heads, key_heads, preferred_element_type=jnp.float32
    ) * (1.0 / math.sqrt(HD))
    rows = row_first + jnp.arange(count_q, dtype=jnp.int32)
    columns = jnp.arange(count_k, dtype=jnp.int32)
    allowed = (
        (owner_rows[:, None] == owner_cols[None, :])
        & (owner_rows[:, None] >= 0)
        & (columns[None, :] <= rows[:, None])
    )
    return (jnp.where(allowed[None, None], scores, NEGATIVE), allowed)


def online_step(carry, queries, keys, values, owner_rows, owner_cols, row_first):
    top, total, accum = carry
    count = keys.shape[0]
    kv_heads = keys.shape[1] // HD
    scores, allowed = block_scores(queries, keys, owner_rows, owner_cols, row_first)
    new_top = jnp.maximum(top, jnp.max(scores, axis=-1))
    weights = jnp.where(allowed[None, None], jnp.exp(scores - new_top[..., None]), 0.0)
    total = jnp.sum(weights, axis=-1)
    value_heads = values.reshape(count, kv_heads, HD)
    mixed = jnp.einsum(
        "kgqt,tkd->qkgd",
        weights.astype(jnp.bfloat16),
        value_heads,
        preferred_element_type=jnp.float32,
    )
    accum = mixed
    return (new_top, total, accum)


def empty_carry(rows, kv_heads, grouped):
    init_top = jnp.full((kv_heads, grouped, rows), NEGATIVE, jnp.float32)
    init_total = jnp.zeros((kv_heads, grouped, rows), jnp.float32)
    init_acc = jnp.zeros((rows, kv_heads, grouped, HD), jnp.float32)
    return (init_top, init_total, init_acc)


def finish(mixed, total, owner_rows):
    live = owner_rows >= 0
    denom = jnp.where(live[None, None, :], total, 1.0)
    result = mixed / jnp.transpose(denom, (2, 0, 1))[..., None]
    result = jnp.where(live[:, None, None, None], result, 0.0)
    return result.reshape(result.shape[0], -1).astype(jnp.bfloat16)


def decode_attend(query_new, key_new, value_new, cache_keys, cache_values, owners):
    requests = query_new.shape[0]
    kv_heads = cache_keys.shape[1] // HD
    grouped = query_new.shape[1] // (HD * kv_heads)
    query_heads = query_new.reshape(requests, kv_heads, grouped, HD)
    key_heads = cache_keys.reshape(cache_keys.shape[0], kv_heads, HD)
    value_heads = cache_values.reshape(cache_values.shape[0], kv_heads, HD)
    scale = 1.0 / math.sqrt(HD)
    scores = (
        jnp.einsum("rkgd,tkd->rkgt", query_heads, key_heads, preferred_element_type=jnp.float32)
        * scale
    )
    own = (
        jnp.einsum(
            "rkgd,rkd->rkg",
            query_heads,
            key_new.reshape(requests, kv_heads, HD),
            preferred_element_type=jnp.float32,
        )
        * scale
    )
    match = owners[None, :] == jnp.arange(requests, dtype=jnp.int32)[:, None]
    scores = jnp.where(match[:, None, None, :], scores, NEGATIVE)
    top = jnp.maximum(jnp.max(scores, axis=-1), own)
    weights = jnp.where(match[:, None, None, :], jnp.exp(scores - top[..., None]), 0.0)
    own_weight = jnp.exp(own - top)
    total = jnp.sum(weights, axis=-1) + own_weight
    mixed = jnp.einsum(
        "rkgt,tkd->rkgd",
        weights.astype(jnp.bfloat16),
        value_heads,
        preferred_element_type=jnp.float32,
    )
    own_value = value_new.reshape(requests, kv_heads, 1, HD).astype(jnp.float32)
    mixed = mixed + own_weight.astype(jnp.bfloat16).astype(jnp.float32)[..., None] * own_value
    return (mixed / total[..., None]).reshape(requests, -1).astype(jnp.bfloat16)


def shards(
    lengths,
    group_of,
    query_pre,
    key_pre,
    value_pre,
    query_new,
    key_new,
    value_new,
    hidden_new,
    out_weight,
    norm_gain,
    gate_weight,
    up_weight,
    down_weight,
):
    seq_count = lax.axis_size("seq")
    seq_index = lax.axis_index("seq")
    group_idx = lax.axis_index("grp")
    tokens_dev = query_pre.shape[0]
    group_slots = tokens_dev * seq_count
    starts = request_starts(lengths, group_of)
    owners = slot_owner(group_idx, starts, lengths, group_of, group_slots)
    cache_keys, cache_values = (
        lax.all_to_all(key_pre, "seq", split_axis=1, concat_axis=0, tiled=True),
        lax.all_to_all(value_pre, "seq", split_axis=1, concat_axis=0, tiled=True),
    )
    my_first = seq_index * tokens_dev
    my_last = my_first + tokens_dev - 1
    owner_rows = lax.dynamic_slice_in_dim(owners, my_first, tokens_dev, 0)
    any_live = jnp.any(owner_rows >= 0)
    grouped = H // KVH
    piece_keys = lax.all_gather(key_pre, "seq", axis=0, tiled=True)
    piece_values = lax.all_gather(value_pre, "seq", axis=0, tiled=True)
    needed = (jnp.int32(0) <= my_last) & any_live

    def attend(state):
        return online_step(state, query_pre, piece_keys, piece_values, owner_rows, owners, my_first)

    def keep(state):
        return state

    top, total, accum = lax.cond(needed, attend, keep, empty_carry(tokens_dev, KVH, grouped))
    prefill_attention = finish(accum, total, owner_rows)
    attended = decode_attend(query_new, key_new, value_new, cache_keys, cache_values, owners)
    mine = group_of == group_idx
    attended = jnp.where(mine[:, None], attended, jnp.zeros_like(attended))
    decode_att = lax.psum(attended, "grp").astype(jnp.float32).astype(jnp.bfloat16)
    proj_part = jnp.dot(decode_att, out_weight, preferred_element_type=jnp.float32)
    projected = lax.psum(proj_part, "seq")
    resid = hidden_new.astype(jnp.float32) + projected
    squares = lax.psum(jnp.sum(resid * resid, axis=-1), "grp")
    normed = (
        resid * lax.rsqrt(squares / D + 1e-05)[:, None] * norm_gain.astype(jnp.float32)[None, :]
    ).astype(jnp.bfloat16)
    gate_part = jnp.dot(normed, gate_weight, preferred_element_type=jnp.float32)
    upper_part = jnp.dot(normed, up_weight, preferred_element_type=jnp.float32)
    gate, upper = lax.psum((gate_part, upper_part), "grp")
    hidden = (jax.nn.silu(gate) * upper).astype(jnp.bfloat16)
    down_part = jnp.dot(hidden, down_weight, preferred_element_type=jnp.float32)
    down_share = lax.psum_scatter(down_part, "seq", scatter_dimension=1, tiled=True)
    width = down_share.shape[1]
    resid_share = lax.dynamic_slice_in_dim(resid, seq_index * width, width, 1)
    decode_hidden = (resid_share + down_share).astype(jnp.bfloat16)
    return (prefill_attention, decode_hidden)


def solution(mesh):
    return jax.shard_map(
        shards,
        mesh=mesh,
        in_specs=(
            P(),
            P(),
            P(("grp", "seq"), None),
            P(("grp", "seq"), None),
            P(("grp", "seq"), None),
            P(None, "seq"),
            P(None, "seq"),
            P(None, "seq"),
            P(None, "grp"),
            P("seq", "grp"),
            P("grp"),
            P("grp", "seq"),
            P("grp", "seq"),
            P("seq", "grp"),
        ),
        out_specs=(P(("grp", "seq"), None), P(None, ("grp", "seq"))),
        check_vma=False,
    )
```

profile of v0, /device:TPU:25, one launch (start us, length us, event | category | flops | bytes accessed | tf_op | source)
XLA Modules:
  0.0 443.3 jit_solution(8444500420966843841)
XLA Ops:
  7.2 1.9 copy.105
  9.1 4.5 %all-to-all-start = ((bf16[256,4,256]{2,0,1:T(8,128)(2,1)}), bf16[256,4,256]{2,0,1:T(8,128)(2,1)S(1)}, u32[]{:S(2)}, u32[]{:S(2)}) async-start(bf16[256,4,256]{2,0,1:T(8,128)(2,1)} %bitcast.89), calls=%async_computation | async-start | bytes 1048576 | tf_op jit(solution)/shard_map/all_to_all | solution.py:151
  13.6 0.7 broadcast_compare_fusion.2
  14.3 0.9 select_reduce_fusion.1
  15.2 0.7 add.64
  15.8 0.8 copy.76
  16.7 0.7 reshape.166
  17.4 0.1 fusion.44
  17.5 0.1 copy.59
  17.6 1.9 copy.104
  19.5 0.1 select_reduce_fusion
  19.6 0.7 copy_bitcast_fusion.3
  20.3 4.5 %all-to-all-done = bf16[256,4,256]{2,0,1:T(8,128)(2,1)S(1)} async-done(((bf16[256,4,256]{2,0,1:T(8,128)(2,1)}), bf16[256,4,256]{2,0,1:T(8,128)(2,1)S(1)}, u32[]{:S(2)}, u32[]{:S(2)}) %all-to-all-start) | async-done | bytes 524320 | tf_op jit(solution)/shard_map/all_to_all | solution.py:151
  24.8 6.2 %all-to-all-start.1 = ((bf16[256,4,256]{2,0,1:T(8,128)(2,1)}), bf16[256,4,256]{2,0,1:T(8,128)(2,1)S(1)}, u32[]{:S(2)}, u32[]{:S(2)}) async-start(bf16[256,4,256]{2,0,1:T(8,128)(2,1)} %bitcast.88), calls=%async_computation.1 | async-start | bytes 1048576 | tf_op jit(solution)/shard_map/all_to_all | solution.py:152
  31.0 0.1 reshape.154
  31.2 0.4 fusion.43
  31.6 0.3 fusion.22
  31.9 10.4 %all-to-all-done.1 = bf16[256,4,256]{2,0,1:T(8,128)(2,1)S(1)} async-done(((bf16[256,4,256]{2,0,1:T(8,128)(2,1)}), bf16[256,4,256]{2,0,1:T(8,128)(2,1)S(1)}, u32[]{:S(2)}, u32[]{:S(2)}) %all-to-all-start.1) | async-done | bytes 524320 | tf_op jit(solution)/shard_map/all_to_all | solution.py:152
  42.3 0.1 reshape.157
  42.4 0.4 fusion.21
  42.8 0.7 bitcast_select_fusion.1
  43.6 54.3 %all-reduce.5.cloned.1.call-done = bf16[16,2048]{1,0:T(8,128)(2,1)} async-done(((bf16[16,2048]{1,0:T(8,128)(2,1)}), bf16[16,2048]{1,0:T(8,128)(2,1)}) %all-reduce.5.cloned.1.call-update) | async-done | bytes 65552 | tf_op jit(solution)/shard_map/psum | solution.py:174
  97.9 3.5 fusion.45
  101.5 31.1 %all-reduce.7.cloned.1.call-done = f32[16,1024]{1,0:T(8,128)} async-done(((f32[16,1024]{1,0:T(8,128)}), f32[16,1024]{1,0:T(8,128)}) %all-reduce.7.cloned.1.call-update) | async-done | bytes 65552 | tf_op jit(solution)/shard_map/psum | solution.py:176
  132.6 1.0 multiply_reduce_fusion
  133.6 13.6 %psum.37 = f32[16]{0:T(128)S(1)} all-reduce(f32[16]{0:T(128)S(1)} %get-tuple-element.28), channel_id=1, replica_groups=mesh['grp'=8,'seq'=4] {'grp'}, use_global_device_ids=true, to_apply=%region_12.13 | all-reduce | flops 16 | bytes 128 | tf_op jit(solution)/shard_map/psum | solution.py:178
  147.2 5.3 %fusion.41 = f32[16,4096]{1,0:T(8,128)} fusion(bf16[1024,4096]{1,0:T(8,128)(2,1)} %param.27, f32[16,1024]{1,0:T(8,128)S(1)} %get-tuple-element.29, f32[1024]{0:T(1024)S(1)} %convert_element_type.66, f32[16]{0:T(128)S(1)} %add_rsqrt_fusion), kind=kOutput, calls=%fused_computation.73 | convolution fusion | flops 134266880 | bytes 8720448 | tf_op jit(solution)/shard_map/dot_general | solution.py:182
  152.6 5.3 %fusion.40 = f32[16,4096]{1,0:T(8,128)} fusion(bf16[1024,4096]{1,0:T(8,128)(2,1)} %param.28, f32[16,1024]{1,0:T(8,128)S(1)} %get-tuple-element.29, f32[1024]{0:T(1024)S(1)} %convert_element_type.66, f32[16]{0:T(128)S(1)} %add_rsqrt_fusion), kind=kOutput, calls=%fused_computation.72 | convolution fusion | flops 134266880 | bytes 8720448 | tf_op jit(solution)/shard_map/dot_general | solution.py:183
  158.0 53.8 %all-reduce.9.cloned.1.call-done = (f32[16,4096]{1,0:T(8,128)}, f32[16,4096]{1,0:T(8,128)}) async-done(((f32[16,4096]{1,0:T(8,128)}, f32[16,4096]{1,0:T(8,128)}), (f32[16,4096]{1,0:T(8,128)}, f32[16,4096]{1,0:T(8,128)})) %all-reduce.9.cloned.1.call-update) | async-done | bytes 524304 | tf_op jit(solution)/shard_map/psum | solution.py:184
  211.8 5.4 %fusion.30 = f32[16,1024]{1,0:T(8,128)} fusion(bf16[4096,1024]{1,0:T(8,128)(2,1)} %param.29, f32[16,4096]{1,0:T(8,128)} %get-tuple-element.26, f32[16,4096]{1,0:T(8,128)} %get-tuple-element.27), kind=kOutput, calls=%fused_computation.40 | convolution fusion | flops 134610944 | bytes 8978432 | tf_op jit(solution)/shard_map/dot_general | solution.py:186
  217.2 0.5 all-gather.3.cloned.1.call-update
  217.8 0.5 all-gather.5.cloned.1.call-update
  218.3 0.7 fusion.42
  219.7 12.4 %reduce-scatter.2.cloned.1.call-done = f32[16,256]{1,0:T(8,128)} async-done(((f32[16,1024]{1,0:T(8,128)}), f32[16,256]{1,0:T(8,128)}) %reduce-scatter.2.cloned.1.call-update) | async-done | bytes 16400 | tf_op jit(solution)/shard_map/reduce_scatter | solution.py:187
  232.1 1.3 add_convert_fusion
  233.4 46.8 %all-gather.3.cloned.1.call-done = bf16[1024,1024]{1,0:T(8,128)(2,1)} async-done(((bf16[256,1024]{1,0:T(8,128)(2,1)}), bf16[1024,1024]{1,0:T(8,128)(2,1)}) %all-gather.3.cloned.1.call-update) | async-done | bytes 2097168 | tf_op jit(solution)/shard_map/all_gather | solution.py:159
  280.2 46.1 %all-gather.5.cloned.1.call-done = bf16[1024,1024]{1,0:T(8,128)(2,1)} async-done(((bf16[256,1024]{1,0:T(8,128)(2,1)}), bf16[1024,1024]{1,0:T(8,128)(2,1)}) %all-gather.5.cloned.1.call-update) | async-done | bytes 2097168 | tf_op jit(solution)/shard_map/all_gather | solution.py:160
  326.3 91.8 %conditional.1 = (f32[8,8,256]{2,1,0:T(8,128)S(1)}, f32[256,8,8,128]{3,0,2,1:T(8,128)}) conditional(s32[]{:T(128)} %convert_element_type.55, () %tuple.16, (s32[256]{0:T(256)S(1)}, s32[1024]{0:T(1024)S(1)}, s32[]{:T(128)}, bf16[1024,1024]{1,0:T(8,128)(2,1)}, bf16[256,8192]{1,0:T(8,128)(2,1)}, /*index=5*/bf16[1024,1024]{1,0:T(8,128)(2,1)}) %tuple.17), branch_computations={%region_3.4_spmd, %region_4.7_spmd} | conditional | flops 8809070592 | bytes 244720176 | solution.py:169
  326.3 0.3 fusion.13
  326.7 5.6 %copy.70 = bf16[32,8,64,128]{3,2,1,0:T(8,128)(2,1)} copy(bf16[32,8,64,128]{3,1,2,0:T(8,128)(2,1)} %bitcast.93) | data formatting | bytes 8388608 | tf_op jit(solution)/shard_map/cond
  332.3 0.6 copy.69
  332.9 30.2 %fusion = (f32[8,8,256]{2,1,0:T(8,128)S(1)}, f32[8,1024,256,8]{2,1,3,0:T(8,128)}) fusion(pred[256,1024]{0,1:T(8,128)(4,1)S(1)} %fusion.13, bf16[256,8,8,128]{3,2,1,0:T(8,128)(2,1)} %bitcast.91, bf16[1024,8,128,1]{2,1,0,3:T(8,128)(2,1)S(1)} %bitcast.92), kind=kOutput, calls=%fused_computation.2 | convolution fusion | flops 4345282560 | bytes 73728000 | tf_op jit(solution)/shard_map/cond/branch_1_fun/qkgd,tkd->kgqt/dot_general | solution.py:42
  363.1 2.2 copy.71
  365.3 30.9 %fusion.8 = f32[256,8,8,128]{3,0,2,1:T(8,128)} fusion(f32[8,1024,256,8]{2,1,3,0:T(8,128)} %get-tuple-element.34, f32[8,8,256]{2,1,0:T(8,128)S(1)} %broadcast_maximum_fusion, pred[256,1024]{0,1:T(8,128)(4,1)S(1)} %fusion.13, bf16[1024,8,128,1]{2,1,0,3:T(8,128)(2,1)S(1)} %bitcast.97), kind=kOutput, calls=%fused_computation.9 | convolution fusion | flops 4378853376 | bytes 77922304 | tf_op jit(solution)/shard_map/cond/branch_1_fun/kgqt,tkd->qkgd/dot_general | solution.py:64
  396.2 21.7 %fusion.2 = f32[8,8,256]{2,1,0:T(8,128)S(1)} fusion(f32[8,1024,256,8]{2,1,3,0:T(8,128)} %get-tuple-element.34, f32[8,8,256]{2,1,0:T(8,128)S(1)} %broadcast_maximum_fusion, pred[256,1024]{0,1:T(8,128)(4,1)S(1)} %fusion.13), kind=kLoop, calls=%fused_computation.4 | loop fusion | flops 83869696 | bytes 67502080 | tf_op jit(solution)/shard_map/cond/branch_1_fun/reduce_sum | solution.py:62
  418.2 5.4 %select_convert_fusion = bf16[256,8,8,128]{3,0,2,1:T(8,128)(2,1)S(1)} fusion(f32[256,8,8,128]{3,0,2,1:T(8,128)} %get-tuple-element.22, f32[256,8,8]{0,2,1:T(8,128)S(1)} %select_bitcast_fusion, pred[256]{0:T(512)(128)(4,1)S(1)} %get-tuple-element.31), kind=kLoop, calls=%fused_computation.20 | loop fusion | flops 6291456 | bytes 12648704 | tf_op jit(solution)/shard_map/convert_element_type | solution.py:86
  423.6 2.7 copy.46
  426.3 10.2 %copy.103 = bf16[32,8,64,128]{3,1,2,0:T(8,128)(2,1)} copy(bf16[32,8,64,128]{3,2,1,0:T(8,128)(2,1)S(1)} %bitcast.90) | data formatting | bytes 8388608
  (28 shorter events, 0.4 us)
Async XLA Ops:
  7.2 94.3 %copy-start.2 = (bf16[1024]{0:T(1024)(128)(2,1)S(1)}, bf16[1024]{0:T(1024)(128)(2,1)}, u32[]{:S(2)}) copy-start(bf16[1024]{0:T(1024)(128)(2,1)} %param.26) | copy-start | bytes 6148
  7.2 125.5 %copy-start.1 = (bf16[16,1024]{1,0:T(8,128)(2,1)S(1)}, bf16[16,1024]{1,0:T(8,128)(2,1)}, u32[]{:S(2)}) copy-start(bf16[16,1024]{1,0:T(8,128)(2,1)} %param.24) | copy-start | bytes 98308
  9.1 15.8 %all-to-all-start = ((bf16[256,4,256]{2,0,1:T(8,128)(2,1)}), bf16[256,4,256]{2,0,1:T(8,128)(2,1)S(1)}, u32[]{:S(2)}, u32[]{:S(2)}) async-start(bf16[256,4,256]{2,0,1:T(8,128)(2,1)} %bitcast.89), calls=%async_computation | async-start | bytes 1048576 | tf_op jit(solution)/shard_map/all_to_all | solution.py:151
  24.8 17.4 %all-to-all-start.1 = ((bf16[256,4,256]{2,0,1:T(8,128)(2,1)}), bf16[256,4,256]{2,0,1:T(8,128)(2,1)S(1)}, u32[]{:S(2)}, u32[]{:S(2)}) async-start(bf16[256,4,256]{2,0,1:T(8,128)(2,1)} %bitcast.88), calls=%async_computation.1 | async-start | bytes 1048576 | tf_op jit(solution)/shard_map/all_to_all | solution.py:152
  31.0 66.8 %all-reduce.5.cloned.1.call-start = ((), (), s32[]{:S(2)}) async-start(), calls=%async_computation.5 | async-start | bytes 131072 | tf_op jit(solution)/shard_map/psum | solution.py:174
  43.5 89.1 %all-reduce.7.cloned.1.call-start = ((), (), s32[]{:S(2)}) async-start(), calls=%async_computation.6 | async-start | bytes 131072 | tf_op jit(solution)/shard_map/psum | solution.py:176
  101.4 110.3 %all-reduce.9.cloned.1.call-start = ((), (), s32[]{:S(2)}) async-start(), calls=%async_computation.8 | async-start | bytes 1048576 | tf_op jit(solution)/shard_map/psum | solution.py:184
  157.9 74.2 %reduce-scatter.2.cloned.1.call-start = ((), (), s32[]{:S(2)}) async-start(), calls=%async_computation.7 | async-start | bytes 81920 | tf_op jit(solution)/shard_map/reduce_scatter | solution.py:187
  217.2 63.0 %all-gather.3.cloned.1.call-start = ((), (), s32[]{:S(2)}) async-start(), calls=%async_computation.3 | async-start | bytes 2621440 | tf_op jit(solution)/shard_map/all_gather | solution.py:159
  217.8 108.6 %all-gather.5.cloned.1.call-start = ((), (), s32[]{:S(2)}) async-start(), calls=%async_computation.4 | async-start | bytes 2621440 | tf_op jit(solution)/shard_map/all_gather | solution.py:160
  326.3 5.9 %copy-start = (bf16[1024,1024]{1,0:T(8,128)(2,1)S(1)}, bf16[1024,1024]{1,0:T(8,128)(2,1)}, u32[]{:S(2)}) copy-start(bf16[1024,1024]{1,0:T(8,128)(2,1)} %get-tuple-element.15) | copy-start | bytes 6291460 | tf_op jit(solution)/shard_map/cond
Sparse Core Ops, SparseCore 0:
  43.7 54.1 all-reduce.4
  101.5 31.0 all-reduce.6
  158.0 53.6 all-reduce.8
  217.3 14.7 reduce-scatter.1
  233.5 46.6 all-gather.2
  281.6 44.6 all-gather.4
where the time goes:
time: 448 us; the launch traced here: 443 us
  waiting for transfers between devices  260 us (58%)
  matrix products  81.5 us (18%)
  other arithmetic  34.6 us (8%)
  local copies, waits for them, and re-layouts  26.9 us (6%)
  between operations  14.9 us (3%)
  blocking collectives  13.6 us (3%)
  starting transfers between devices  11 us (2%)
    psum x1, waiting for transfers between devices, shards(): lax.psum(attended, 'grp').astype(jnp.float32).astype(jnp.bfloat16)  54.3 us
    psum x1, waiting for transfers between devices, shards(): gate, upper = lax.psum((gate_part, upper_part), 'grp')  53.8 us
    all_gather x1, waiting for transfers between devices, shards(): piece_keys = lax.all_gather(key_pre, 'seq', axis=0, tiled=True)  46.8 us
    all_gather x1, waiting for transfers between devices, shards(): piece_values = lax.all_gather(value_pre, 'seq', axis=0, tiled=True)  46.1 us
    psum x1, waiting for transfers between devices, shards(): projected = lax.psum(proj_part, 'seq')  31.1 us
    dot_general x1, matrix products, online_step(): jnp.einsum('kgqt,tkd->qkgd', weights.astype(jnp.bfloat16), value_heads, p...  30.9 us
    dot_general x1, matrix products, block_scores(): jnp.einsum('qkgd,tkd->kgqt', query_heads, key_heads, preferred_element_ty...  30.2 us
    reduce_sum x1, other arithmetic, online_step(): total = jnp.sum(weights, axis=-1)  21.7 us
  transfers between devices with their start and end apart: 8, of which 8 were waited for; matrix products, arithmetic and copies ran while one was open for 2% of the time, Pallas kernels for 0%

commit v1 on v0

v1 whole, which is shorter than its diff:
```python
import functools
import math

import jax
import jax.numpy as jnp
from jax import lax
from jax.experimental import pallas as pl
from jax.experimental.pallas import tpu as pltpu
from jax.sharding import PartitionSpec as P

HD = 128
Q_PER_KV = 8
MAX_IN_GROUP = 3
SLOTS_R = 4
NEGATIVE = -1e30
LOG2E = 1.4426950408889634
MIB = 1 << 20

F32 = jnp.float32
BF16 = jnp.bfloat16


def dot(a, b):
    return jnp.dot(a, b, preferred_element_type=F32)


def dot_t(a, b):
    return lax.dot_general(a, b, (((1,), (1,)), ((), ())), preferred_element_type=F32)


def plan(lengths, groups, group):
    ids = [jnp.int32(-1)] * MAX_IN_GROUP
    first = [jnp.int32(0)] * MAX_IN_GROUP
    end = [jnp.int32(0)] * MAX_IN_GROUP
    count = jnp.int32(0)
    used = jnp.int32(0)
    for r in range(lengths.shape[0]):
        mine = groups[r] == group
        length = lengths[r]
        for k in range(MAX_IN_GROUP):
            here = mine & (count == k)
            ids[k] = jnp.where(here, r, ids[k])
            first[k] = jnp.where(here, used, first[k])
            end[k] = jnp.where(here, used + length, end[k])
        count = count + jnp.where(mine, 1, 0)
        used = used + jnp.where(mine, length, 0)
    return ids, first, end


def pick_rows(ids, rows, columns):
    row = lax.broadcasted_iota(jnp.int32, (rows, columns), 0)
    column = lax.broadcasted_iota(jnp.int32, (rows, columns), 1)
    target = jnp.full((rows, columns), -1, jnp.int32)
    for k in range(MAX_IN_GROUP):
        target = jnp.where(row == k, ids[k], target)
    return jnp.where(column == target, 1.0, 0.0).astype(BF16)


def split3(x):
    hi = x.astype(BF16)
    rest = x - hi.astype(F32)
    mid = rest.astype(BF16)
    low = (rest - mid.astype(F32)).astype(BF16)
    return hi, mid, low


def select_kernel(lengths, groups, pos, query_ref, out_ref):
    ids, _, _ = plan(lengths, groups, pos[0])
    pick = pick_rows(ids, 8, query_ref.shape[0])
    out_ref[...] = dot(pick, query_ref[...])[:SLOTS_R].astype(BF16)


def partial_kernel(n, lengths, groups, pos, *refs):
    queries, (key_ref, value_ref), outs = refs[:n], refs[n : n + 2], refs[n + 2 :]
    _, first, end = plan(lengths, groups, pos[0])
    tokens = key_ref.shape[0]
    kv_per = queries[0].shape[1] // (HD * Q_PER_KV)
    rows = Q_PER_KV * SLOTS_R
    slot = pos[1] * tokens + lax.broadcasted_iota(jnp.int32, (rows, tokens), 1)
    rank = lax.broadcasted_iota(jnp.int32, (rows, tokens), 0) & (SLOTS_R - 1)
    low = jnp.zeros((rows, tokens), jnp.int32)
    high = jnp.zeros((rows, tokens), jnp.int32)
    for k in range(MAX_IN_GROUP):
        low = jnp.where(rank == k, first[k], low)
        high = jnp.where(rank == k, end[k], high)
    allowed = (slot >= low) & (slot < high)
    lane = lax.broadcasted_iota(jnp.int32, (rows, HD), 1)
    scale = 1.0 / math.sqrt(HD)
    for t in range(n):
        shard = lax.rem(pos[1] - t + n, n)
        query = queries[t][...].astype(F32)
        for i in range(kv_per):
            columns = pl.ds(pl.multiple_of((shard * kv_per + i) * HD, HD), HD)
            keys = key_ref[:, columns]
            values = value_ref[:, columns]
            heads = [query[:, (i * Q_PER_KV + h) * HD :][:, :HD] for h in range(Q_PER_KV)]
            stacked = jnp.concatenate(heads, axis=0).astype(BF16)
            scores = jnp.where(allowed, dot_t(stacked, keys) * scale, NEGATIVE)
            top = jnp.max(scores, axis=1, keepdims=True)
            weights = jnp.where(allowed, jnp.exp(scores - top), 0.0)
            total = jnp.sum(weights, axis=1, keepdims=True)
            some = total > 0.0
            mixed = dot(weights.astype(BF16), values) / jnp.where(some, total, 1.0)
            level = jnp.where(some, top + jnp.log(jnp.where(some, total, 1.0)), NEGATIVE)
            hi, mid, rest = split3(jnp.broadcast_to(level, (rows, HD)))
            stats = jnp.where(
                lane < 32, hi.astype(F32), jnp.where(lane < 64, mid.astype(F32), rest.astype(F32))
            )
            outs[t][i * rows : (i + 1) * rows, :] = jnp.concatenate([mixed, stats], axis=1).astype(
                BF16
            )


def combine_kernel(n, lengths, groups, pos, *refs):
    parts, (query_ref, key_ref, value_ref, out_ref) = refs[:n], refs[n:]
    ids, _, _ = plan(lengths, groups, pos[0])
    heads = query_ref.shape[1] // HD
    pick = pick_rows(ids, 8, key_ref.shape[0])
    keys = dot(pick, key_ref[...])[:SLOTS_R]
    values = dot(pick, value_ref[...])[:SLOTS_R]
    query = query_ref[...].astype(F32)

    def by_head(array, group):
        return jnp.concatenate(
            [array[:, (h // group) * HD :][:, :HD] for h in range(heads)], axis=0
        )

    own_score = jnp.sum(
        by_head(query, 1) * by_head(keys, Q_PER_KV), axis=1, keepdims=True
    ) * (1.0 / math.sqrt(HD))
    own_value = by_head(values, Q_PER_KV)
    mixes = []
    levels = []
    top = own_score
    for t in range(n):
        part = parts[t][...].astype(F32)
        stats = part[:, HD:]
        level = stats[:, 0:1] + stats[:, 32:33] + stats[:, 64:65]
        mixes.append(part[:, :HD])
        levels.append(level)
        top = jnp.maximum(top, level)
    own_weight = jnp.exp(own_score - top)
    total = own_weight
    mixed = own_weight.astype(BF16).astype(F32) * own_value
    for t in range(n):
        weight = jnp.exp(levels[t] - top)
        total = total + weight
        mixed = mixed + weight * mixes[t]
    result = mixed / total
    for h in range(heads):
        out_ref[:, h * HD : (h + 1) * HD] = result[h * SLOTS_R : (h + 1) * SLOTS_R].astype(BF16)


def project_kernel(count, pos, pick_ref, *refs):
    parts, (weight_ref, out_ref, att_ref, sum_ref) = refs[:count], refs[count:]
    step = pl.program_id(0)
    depth = weight_ref.shape[0]

    @pl.when(step == 0)
    def _():
        stacked = jnp.concatenate([part[...].astype(F32) for part in parts], axis=0).astype(BF16)
        att = dot(pick_ref[...], stacked).astype(BF16)
        for j in range(att_ref.shape[0]):
            att_ref[j] = att[:, j * depth : (j + 1) * depth]
        sum_ref[...] = jnp.zeros_like(sum_ref)

    sum_ref[...] += dot(att_ref[step], weight_ref[...])

    @pl.when(step == pl.num_programs(0) - 1)
    def _():
        out_ref[...] = sum_ref[...].astype(out_ref.dtype)


def gate_up_kernel(n, count, pos, *refs):
    parts, (hidden_ref, gain_ref, gate_ref, up_ref), outs = (
        refs[:n],
        refs[n : n + 4],
        refs[n + 4 :],
    )
    resid_ref, sends, scaled_ref = outs[0], outs[1 : 1 + count], outs[1 + count]
    step = pl.program_id(0)
    width = gate_ref.shape[1]

    @pl.when(step == 0)
    def _():
        resid = parts[0][...].astype(F32)
        for part in parts[1:]:
            resid = resid + part[...].astype(F32)
        resid = resid + hidden_ref[...].astype(F32)
        resid_ref[...] = resid
        scaled_ref[...] = (resid * gain_ref[...].astype(F32)).astype(BF16)
        squares = jnp.sum(resid * resid, axis=1, keepdims=True)
        rows = resid.shape[0]
        hi, mid, low = split3(jnp.broadcast_to(squares, (rows, HD)))
        lane = lax.broadcasted_iota(jnp.int32, (rows, HD), 1)
        stats = jnp.where(
            lane < 32, hi.astype(F32), jnp.where(lane < 64, mid.astype(F32), low.astype(F32))
        )
        for t in range(count):
            sends[t][:, 2 * width :] = stats.astype(BF16)

    scaled = scaled_ref[...]
    gate = dot(scaled, gate_ref[...]).astype(BF16)
    upper = dot(scaled, up_ref[...]).astype(BF16)
    for t in range(count):

        @pl.when(step == t)
        def _():
            sends[t][:, :width] = gate
            sends[t][:, width : 2 * width] = upper


def hidden_kernel(count, features, *refs):
    parts, out_ref = refs[:count], refs[count]
    width = out_ref.shape[1]
    total = parts[0][...].astype(F32)
    for part in parts[1:]:
        total = total + part[...].astype(F32)
    stats = total[:, 2 * width :]
    squares = stats[:, 0:1] + stats[:, 32:33] + stats[:, 64:65]
    inverse = lax.rsqrt(squares / features + 1e-05)
    gate = total[:, :width] * inverse
    upper = total[:, width : 2 * width] * inverse
    out_ref[...] = (gate / (1.0 + jnp.exp(-gate)) * upper).astype(BF16)


def down_kernel(count, n, pos, *refs):
    parts, weight_ref, sends, sum_ref = (
        refs[:count],
        refs[count],
        refs[count + 1 : count + 1 + n],
        refs[count + 1 + n],
    )
    step = pl.program_id(0)
    width = sends[0].shape[1]

    @pl.when(step == 0)
    def _():
        sum_ref[...] = jnp.zeros_like(sum_ref)

    for t in range(count):

        @pl.when(step == t)
        def _():
            sum_ref[...] += dot(parts[t][...], weight_ref[...])

    @pl.when(step == count - 1)
    def _():
        for own in range(n):

            @pl.when(pos[1] == own)
            def _():
                for t in range(n):
                    target = (own + t) % n
                    sends[t][...] = sum_ref[:, target * width : (target + 1) * width]


def prefill_kernel(n, lengths, groups, pos, *refs):
    query_ref, keys, values, out_ref, bias_ref, key_ref, value_ref = (
        refs[0],
        refs[1 : 1 + n],
        refs[1 + n : 1 + 2 * n],
        refs[1 + 2 * n],
        refs[2 + 2 * n],
        refs[3 + 2 * n],
        refs[4 + 2 * n],
    )
    tokens = query_ref.shape[0]
    _, first, end = plan(lengths, groups, pos[0])
    row_first = pos[1] * tokens
    lowest = row_first + tokens
    for k in range(MAX_IN_GROUP):
        meets = (end[k] > row_first) & (first[k] < row_first + tokens)
        lowest = jnp.where(meets, jnp.minimum(lowest, first[k]), lowest)
    needed = pos[1] - lowest // tokens + 1

    @pl.when(pl.program_id(0) == 0)
    def _():
        row = row_first + lax.broadcasted_iota(jnp.int32, (tokens, tokens), 0)
        column = lax.broadcasted_iota(jnp.int32, (tokens, tokens), 1)
        low = jnp.full((tokens, tokens), 1 << 30, jnp.int32)
        for k in range(MAX_IN_GROUP):
            low = jnp.where((row >= first[k]) & (row < end[k]), first[k], low)
        for t in range(n):
            slot = (pos[1] - t) * tokens + column
            bias_ref[:, t * tokens : (t + 1) * tokens] = jnp.where(
                (slot >= low) & (slot <= row), 0.0, NEGATIVE
            )
        value_ref[:, HD:] = jnp.ones((n * tokens, HD), BF16)

    for t in range(n):
        key_ref[t * tokens : (t + 1) * tokens, :] = keys[t][...]
        value_ref[t * tokens : (t + 1) * tokens, :HD] = values[t][...]

    @pl.when(needed == 0)
    def _():
        out_ref[...] = jnp.zeros_like(out_ref)

    row = row_first + lax.broadcasted_iota(jnp.int32, (tokens, HD), 0)
    live = row < 0
    for k in range(MAX_IN_GROUP):
        live = live | ((row >= first[k]) & (row < end[k]))
    constant = LOG2E / math.sqrt(HD)
    for count in range(1, n + 1):

        @pl.when(needed == count)
        def _():
            def head(h, carry):
                columns = pl.ds(pl.multiple_of(h * HD, HD), HD)
                scores = dot_t(query_ref[:, columns], key_ref[: count * tokens, :])
                scores = scores * constant + bias_ref[:, : count * tokens]
                top = jnp.max(scores, axis=1, keepdims=True)
                weights = jnp.exp2(scores - top).astype(BF16)
                mixed = dot(weights, value_ref[: count * tokens, :])
                result = mixed[:, :HD] / mixed[:, HD:]
                out_ref[:, columns] = jnp.where(live, result, 0.0).astype(BF16)
                return carry

            lax.fori_loop(0, Q_PER_KV, head, 0, unroll=2)


def call(body, scalars, args, outs, *, grid=None, in_specs=None, out_specs=None, scratch=(), cost, vmem=32):
    whole = pl.BlockSpec(memory_space=pltpu.VMEM)
    if grid is None:
        grid = (1,)
    flops, exps = cost
    moved = sum(a.size * a.dtype.itemsize for a in args) + sum(
        o.size * o.dtype.itemsize for o in outs
    )
    return pl.pallas_call(
        body,
        out_shape=list(outs),
        grid_spec=pltpu.PrefetchScalarGridSpec(
            num_scalar_prefetch=len(scalars),
            grid=grid,
            in_specs=in_specs or [whole] * len(args),
            out_specs=out_specs or [whole] * len(outs),
            scratch_shapes=list(scratch),
        ),
        compiler_params=pltpu.CompilerParams(
            dimension_semantics=("arbitrary",) * len(grid), vmem_limit_bytes=vmem * MIB
        ),
        cost_estimate=pl.CostEstimate(flops=flops, bytes_accessed=moved, transcendentals=exps),
    )(*scalars, *args)


def shift(x, axis, count, t):
    return lax.ppermute(x, axis, [(i, (i + t) % count) for i in range(count)])


def shards(
    lengths,
    group_of,
    query_pre,
    key_pre,
    value_pre,
    query_new,
    key_new,
    value_new,
    hidden_new,
    out_weight,
    norm_gain,
    gate_weight,
    up_weight,
    down_weight,
):
    n = lax.axis_size("seq")
    count = lax.axis_size("grp")
    seq = lax.axis_index("seq").astype(jnp.int32)
    group = lax.axis_index("grp").astype(jnp.int32)
    tokens = query_pre.shape[0]
    reqs = query_new.shape[0]
    kv_heads = key_pre.shape[1] // HD
    shard_width = query_new.shape[1]
    shard_heads = shard_width // HD
    columns = out_weight.shape[1]
    shape = jax.ShapeDtypeStruct
    vmem = pl.BlockSpec(memory_space=pltpu.VMEM)
    pos = jnp.stack([group, seq])
    scalars = (lengths, group_of, pos)

    keys, values = [key_pre], [value_pre]
    for t in range(1, n):
        hops = [(i, i + 1) for i in range(t - 1, n - 1)]
        keys.append(lax.ppermute(keys[-1], "seq", hops))
        values.append(lax.ppermute(values[-1], "seq", hops))

    (query,) = call(
        select_kernel,
        scalars,
        (query_new,),
        (shape((SLOTS_R, shard_width), BF16),),
        cost=(2 * 8 * reqs * shard_width, 0),
    )
    queries = [query] + [shift(query, "seq", n, t) for t in range(1, n)]
    rows = shard_heads * SLOTS_R
    partials = call(
        functools.partial(partial_kernel, n),
        scalars,
        (*queries, key_pre, value_pre),
        [shape((rows, 2 * HD), BF16)] * n,
        cost=(4 * n * rows * tokens * HD, n * rows * tokens),
    )
    partials = [partials[0]] + [shift(partials[t], "seq", n, n - t) for t in range(1, n)]
    (att,) = call(
        functools.partial(combine_kernel, n),
        scalars,
        (*partials, query, key_new, value_new),
        (shape((SLOTS_R, shard_width), BF16),),
        cost=(8 * n * rows * HD, n * rows),
    )
    atts = [att] + [shift(att, "grp", count, t) for t in range(1, count)]

    index = jnp.arange(reqs, dtype=jnp.int32)
    same = group_of[None, :] == group_of[:, None]
    rank = jnp.sum(jnp.where(same & (index[None, :] < index[:, None]), 1, 0), axis=1)
    place = lax.rem(group - group_of + count, count) * SLOTS_R + rank
    pick = (place[:, None] == jnp.arange(count * SLOTS_R, dtype=jnp.int32)[None, :]).astype(BF16)
    steps = 4
    depth = shard_width // steps
    (proj,) = call(
        functools.partial(project_kernel, count),
        (pos,),
        (pick, *atts, out_weight),
        (shape((reqs, columns), BF16),),
        grid=(steps,),
        in_specs=[vmem] * (1 + count) + [pl.BlockSpec((depth, columns), lambda j, p: (j, 0))],
        scratch=(pltpu.VMEM((steps, reqs, depth), BF16), pltpu.VMEM((reqs, columns), F32)),
        cost=(2 * reqs * shard_width * columns, 0),
    )
    projs = [proj] + [shift(proj, "seq", n, t) for t in range(1, n)]

    hidden_shard = gate_weight.shape[1]
    width = hidden_shard // count
    ahead = pl.BlockSpec((columns, width), lambda j, p: (0, lax.rem(p[0] + j, count)))
    resid, *terms = call(
        functools.partial(gate_up_kernel, n, count),
        (pos,),
        (*projs, hidden_new, norm_gain.reshape(1, -1), gate_weight, up_weight),
        [shape((reqs, columns), F32)] + [shape((reqs, 2 * width + HD), BF16)] * count,
        grid=(count,),
        in_specs=[vmem] * (n + 2) + [ahead, ahead],
        scratch=(pltpu.VMEM((reqs, columns), BF16),),
        cost=(4 * reqs * columns * hidden_shard, 0),
    )
    terms = [terms[0]] + [shift(terms[t], "grp", count, t) for t in range(1, count)]
    (hidden,) = call(
        functools.partial(hidden_kernel, count, columns * count),
        (),
        terms,
        (shape((reqs, width), BF16),),
        cost=(8 * count * reqs * width, reqs * width),
    )
    hiddens = [hidden] + [shift(hidden, "grp", count, t) for t in range(1, count)]
    share = columns // n
    downs = call(
        functools.partial(down_kernel, count, n),
        (pos,),
        (*hiddens, down_weight),
        [shape((reqs, share), F32)] * n,
        grid=(count,),
        in_specs=[vmem] * count
        + [pl.BlockSpec((width, columns), lambda j, p: (lax.rem(p[0] - j + count, count), 0))],
        scratch=(pltpu.VMEM((reqs, columns), F32),),
        cost=(2 * reqs * columns * hidden_shard, 0),
    )
    total = lax.dynamic_slice_in_dim(resid, seq * share, share, 1) + downs[0]
    for t in range(1, n):
        total = total + shift(downs[t], "seq", n, t)
    decode_hidden = total.astype(BF16)

    wide = Q_PER_KV * HD
    (prefill,) = call(
        functools.partial(prefill_kernel, n),
        scalars,
        (query_pre, *keys, *values),
        (shape(query_pre.shape, BF16),),
        grid=(kv_heads,),
        in_specs=[pl.BlockSpec((tokens, wide), lambda h, *_: (0, h))]
        + [pl.BlockSpec((tokens, HD), lambda h, *_: (0, h))] * (2 * n),
        out_specs=[pl.BlockSpec((tokens, wide), lambda h, *_: (0, h))],
        scratch=(
            pltpu.VMEM((tokens, n * tokens), F32),
            pltpu.VMEM((n * tokens, HD), BF16),
            pltpu.VMEM((n * tokens, 2 * HD), BF16),
        ),
        cost=(8 * n * tokens * query_pre.size, n * tokens * query_pre.size // HD),
        vmem=40,
    )
    return (prefill, decode_hidden)


def solution(mesh):
    return jax.shard_map(
        shards,
        mesh=mesh,
        in_specs=(
            P(),
            P(),
            P(("grp", "seq"), None),
            P(("grp", "seq"), None),
            P(("grp", "seq"), None),
            P(None, "seq"),
            P(None, "seq"),
            P(None, "seq"),
            P(None, "grp"),
            P("seq", "grp"),
            P("grp"),
            P("grp", "seq"),
            P("grp", "seq"),
            P("seq", "grp"),
        ),
        out_specs=(P(("grp", "seq"), None), P(None, ("grp", "seq"))),
        check_vma=False,
    )
```

time: 448 us -> 194 us (0.43)
  the two profiles are of different devices: /device:TPU:25 before, /device:TPU:31 now
where the time goes in v1:
time: 194 us; the launch traced here: 192 us
  waiting for transfers between devices  65.6 us (34%)
  Pallas kernels  58.1 us (30%)
  starting transfers between devices  47.2 us (24%)
  local copies, waits for them, and re-layouts  19.5 us (10%)
    pallas_call x8, Pallas kernels, call(): pl.pallas_call(body, out_shape=list(outs), grid_spec=pltpu.PrefetchScalar...  58.1 us
    ppermute x33, waiting for transfers between devices, shift(): return lax.ppermute(x, axis, [(i, (i + t) % count) for i in range(count)])  43.4 us
    ppermute x33, starting transfers between devices, shift(): return lax.ppermute(x, axis, [(i, (i + t) % count) for i in range(count)])  39.5 us
    unnamed x38, local copies, waits for them, and re-layouts  18.8 us
    ppermute x3, waiting for transfers between devices, shards(): keys.append(lax.ppermute(keys[-1], 'seq', hops))  12.3 us
    ppermute x3, waiting for transfers between devices, shards(): values.append(lax.ppermute(values[-1], 'seq', hops))  9.95 us
  transfers between devices with their start and end apart: 39, of which 17 were waited for; matrix products, arithmetic and copies ran while one was open for 1% of the time, Pallas kernels for 7%

profile of v1, /device:TPU:31, one launch (start us, length us, event | category | flops | bytes accessed | tf_op | source)
XLA Modules:
  0.0 192.3 jit_solution(8519886390938380180)
XLA Ops:
  0.6 1.3 collective-permute-start
  1.9 1.3 collective-permute-start.3
  3.2 12.3 %collective-permute-done.refs_2_ = bf16[256,1024]{1,0:T(8,128)(2,1)S(1)} collective-permute-done((bf16[256,1024]{1,0:T(8,128)(2,1)}, bf16[256,1024]{1,0:T(8,128)(2,1)S(1)}, u32[]{:S(2)}, u32[]{:S(2)}) %collective-permute-start) | collective-permute-done | bytes 524320 | tf_op jit(solution)/shard_map/ppermute | solution.py:385
  15.5 1.3 collective-permute-start.1
  16.8 9.9 %collective-permute-done.3.refs_6_ = bf16[256,1024]{1,0:T(8,128)(2,1)S(1)} collective-permute-done((bf16[256,1024]{1,0:T(8,128)(2,1)}, bf16[256,1024]{1,0:T(8,128)(2,1)S(1)}, u32[]{:S(2)}, u32[]{:S(2)}) %collective-permute-start.3) | collective-permute-done | bytes 524320 | tf_op jit(solution)/shard_map/ppermute | solution.py:386
  26.8 1.3 collective-permute-start.4
  28.1 0.8 copy-done.8
  31.1 3.3 %collective-permute-start.7 = (bf16[4,2048]{1,0:T(4,128)(2,1)S(1)}, bf16[4,2048]{1,0:T(4,128)(2,1)S(1)}, u32[]{:S(2)}, u32[]{:S(2)}) collective-permute-start(bf16[4,2048]{1,0:T(4,128)(2,1)S(1)} %shard_map.150.refs_0_.refs_4_), channel_id=1, source_target_pairs={{0,2},{1,3},{2,0},{3,1},{4,6},{5,7},{6,4},{7,5},{8,10},{9,11},{10,... | collective-permute-start | bytes 49160 | tf_op jit(solution)/shard_map/ppermute | solution.py:348
  34.5 15.4 %collective-permute-done.6.refs_1_ = bf16[4,2048]{1,0:T(4,128)(2,1)S(1)} collective-permute-done((bf16[4,2048]{1,0:T(4,128)(2,1)S(1)}, bf16[4,2048]{1,0:T(4,128)(2,1)S(1)}, u32[]{:S(2)}, u32[]{:S(2)}) %collective-permute-start.6) | collective-permute-done | bytes 16416 | tf_op jit(solution)/shard_map/ppermute | solution.py:348
  50.2 1.0 copy-done.4
  51.3 1.0 copy-done.6
  53.6 2.6 %shard_map.151 = (bf16[64,256]{1,0:T(8,128)(2,1)S(1)}, bf16[64,256]{1,0:T(8,128)(2,1)S(1)}, bf16[64,256]{1,0:T(8,128)(2,1)S(1)}, bf16[64,256]{1,0:T(8,128)(2,1)S(1)}) custom-call(s32[16]{0:T(128)S(1)} %copy-done.16, s32[16]{0:T(128)S(1)} %copy-done.11, s32[2]{0:T(128)S(1)} %pad_add_fusion.pos, bf16[4,2048]{1,0:T(4,128)(2,1)S(1)} %shard_map.150.refs_0_.refs_4_, ...), custom_call_target="tpu_custom_call" | custom-call | flops 33554432 | bytes 1245184 | tf_op jit(solution)/shard_map/pallas_call | solution.py:330
  56.5 3.0 %collective-permute-start.11 = (bf16[64,256]{1,0:T(8,128)(2,1)S(1)}, bf16[64,256]{1,0:T(8,128)(2,1)S(1)}, u32[]{:S(2)}, u32[]{:S(2)}) collective-permute-start(bf16[64,256]{1,0:T(8,128)(2,1)S(1)} %get-tuple-element.22), channel_id=1, source_target_pairs={{0,1},{1,2},{2,3},{3,0},{4,5},{5,6},{6,7},{7,4},{8,9},{9,10},{10,1... | collective-permute-start | bytes 98312 | tf_op jit(solution)/shard_map/ppermute | solution.py:348
  59.5 1.3 collective-permute-done.9.refs_1_
  62.6 0.9 shard_map.152.refs_0_
  63.5 3.3 %collective-permute-start.12 = (bf16[4,2048]{1,0:T(4,128)(2,1)S(1)}, bf16[4,2048]{1,0:T(4,128)(2,1)S(1)}, u32[]{:S(2)}, u32[]{:S(2)}) collective-permute-start(bf16[4,2048]{1,0:T(4,128)(2,1)S(1)} %shard_map.152.refs_0_), channel_id=1, source_target_pairs={{0,4},{4,8},{8,12},{12,16},{16,20},{20,24},{24,28},{28,0},{1,5},{5... | collective-permute-start | bytes 49160 | tf_op jit(solution)/shard_map/ppermute | solution.py:348
  67.0 1.3 collective-permute-start.13
  68.6 0.9 collective-permute-start.15
  69.7 2.1 %collective-permute-start.16 = (bf16[4,2048]{1,0:T(4,128)(2,1)S(1)}, bf16[4,2048]{1,0:T(4,128)(2,1)S(1)}, u32[]{:S(2)}, u32[]{:S(2)}) collective-permute-start(bf16[4,2048]{1,0:T(4,128)(2,1)S(1)} %shard_map.152.refs_0_), channel_id=1, source_target_pairs={{0,20},{4,24},{8,28},{12,0},{16,4},{20,8},{24,12},{28,16},{1,21},{... | collective-permute-start | bytes 49160 | tf_op jit(solution)/shard_map/ppermute | solution.py:348
  71.8 1.0 collective-permute-start.17
  72.8 0.9 collective-permute-start.18
  73.7 1.3 collective-permute-start.2
  75.0 1.3 collective-permute-start.5
  76.9 2.2 %copy-done.3 = bf16[2048,1024]{1,0:T(8,128)(2,1)S(1)} copy-done((bf16[2048,1024]{1,0:T(8,128)(2,1)S(1)}, bf16[2048,1024]{1,0:T(8,128)(2,1)}, u32[]{:S(2)}) %copy-start.3) | copy-done | bytes 4194328
  79.1 1.7 shard_map.153.refs_0_
  80.8 3.0 %collective-permute-start.19 = (bf16[16,1024]{1,0:T(8,128)(2,1)S(1)}, bf16[16,1024]{1,0:T(8,128)(2,1)S(1)}, u32[]{:S(2)}, u32[]{:S(2)}) collective-permute-start(bf16[16,1024]{1,0:T(8,128)(2,1)S(1)} %shard_map.153.refs_0_), channel_id=1, source_target_pairs={{0,1},{1,2},{2,3},{3,0},{4,5},{5,6},{6,7},{7,4},{8,9},{9,10},{10,1... | collective-permute-start | bytes 98312 | tf_op jit(solution)/shard_map/ppermute | solution.py:348
  83.8 1.4 collective-permute-start.20
  85.9 15.9 %collective-permute-done.19.refs_1_ = bf16[16,1024]{1,0:T(8,128)(2,1)S(1)} collective-permute-done((bf16[16,1024]{1,0:T(8,128)(2,1)S(1)}, bf16[16,1024]{1,0:T(8,128)(2,1)S(1)}, u32[]{:S(2)}, u32[]{:S(2)}) %collective-permute-start.19) | collective-permute-done | bytes 32800 | tf_op jit(solution)/shard_map/ppermute | solution.py:348
  101.8 3.4 %copy-done = bf16[1024,4096]{1,0:T(8,128)(2,1)S(1)} copy-done((bf16[1024,4096]{1,0:T(8,128)(2,1)S(1)}, bf16[1024,4096]{1,0:T(8,128)(2,1)}, u32[]{:S(2)}) %copy-start) | copy-done | bytes 8388632
  105.2 3.4 %copy-done.1 = bf16[1024,4096]{1,0:T(8,128)(2,1)S(1)} copy-done((bf16[1024,4096]{1,0:T(8,128)(2,1)S(1)}, bf16[1024,4096]{1,0:T(8,128)(2,1)}, u32[]{:S(2)}) %copy-start.1) | copy-done | bytes 8388632
  108.5 0.8 copy-done.9
  109.3 5.1 %shard_map.154 = (f32[16,1024]{1,0:T(8,128)S(1)}, bf16[16,1152]{1,0:T(8,128)(2,1)S(1)}, bf16[16,1152]{1,0:T(8,128)(2,1)S(1)}, bf16[16,1152]{1,0:T(8,128)(2,1)S(1...) custom-call(s32[2]{0:T(128)S(1)} %pad_add_fusion.pos, ...), custom_call_target="tpu_custom_call" | custom-call | flops 268435456 | bytes 17303552 | tf_op jit(solution)/shard_map/pallas_call | solution.py:330
  114.5 2.6 %collective-permute-start.22 = (bf16[16,1152]{1,0:T(8,128)(2,1)S(1)}, bf16[16,1152]{1,0:T(8,128)(2,1)S(1)}, u32[]{:S(2)}, u32[]{:S(2)}) collective-permute-start(bf16[16,1152]{1,0:T(8,128)(2,1)S(1)} %get-tuple-element.25), channel_id=1, source_target_pairs={{0,4},{4,8},{8,12},{12,16},{16,20},{20,24},{24,28},{28,0},{1,5},{5... | collective-permute-start | bytes 110600 | tf_op jit(solution)/shard_map/ppermute | solution.py:348
  117.4 1.2 collective-permute-start.24
  119.3 0.9 collective-permute-done.23.refs_2_
  120.2 2.0 %collective-permute-start.26 = (bf16[16,1152]{1,0:T(8,128)(2,1)S(1)}, bf16[16,1152]{1,0:T(8,128)(2,1)S(1)}, u32[]{:S(2)}, u32[]{:S(2)}) collective-permute-start(bf16[16,1152]{1,0:T(8,128)(2,1)S(1)} %get-tuple-element.29), channel_id=1, source_target_pairs={{0,20},{4,24},{8,28},{12,0},{16,4},{20,8},{24,12},{28,16},{1,21},{... | collective-permute-start | bytes 110600 | tf_op jit(solution)/shard_map/ppermute | solution.py:348
  122.8 0.9 collective-permute-start.28
  123.8 2.7 %collective-permute-done.27.refs_6_ = bf16[16,1152]{1,0:T(8,128)(2,1)S(1)} collective-permute-done((bf16[16,1152]{1,0:T(8,128)(2,1)S(1)}, bf16[16,1152]{1,0:T(8,128)(2,1)S(1)}, u32[]{:S(2)}, u32[]{:S(2)}) %collective-permute-start.27) | collective-permute-done | bytes 36896 | tf_op jit(solution)/shard_map/ppermute | solution.py:348
  128.3 1.5 collective-permute-start.31
  130.3 2.6 %collective-permute-start.33 = (bf16[16,512]{1,0:T(8,128)(2,1)S(1)}, bf16[16,512]{1,0:T(8,128)(2,1)S(1)}, u32[]{:S(2)}, u32[]{:S(2)}) collective-permute-start(bf16[16,512]{1,0:T(8,128)(2,1)S(1)} %shard_map.155.refs_0_), channel_id=1, source_target_pairs={{0,20},{4,24},{8,28},{12,0},{16,4},{20,8},{24,12},{28,16},{1,21},{... | collective-permute-start | bytes 49160 | tf_op jit(solution)/shard_map/ppermute | solution.py:348
  132.9 0.9 collective-permute-start.34
  134.1 2.3 %collective-permute-done.34.refs_6_ = bf16[16,512]{1,0:T(8,128)(2,1)S(1)} collective-permute-done((bf16[16,512]{1,0:T(8,128)(2,1)S(1)}, bf16[16,512]{1,0:T(8,128)(2,1)S(1)}, u32[]{:S(2)}, u32[]{:S(2)}) %collective-permute-start.34) | collective-permute-done | bytes 16416 | tf_op jit(solution)/shard_map/ppermute | solution.py:348
  136.4 1.4 collective-permute-done.35.refs_7_
  137.9 2.6 %shard_map.156 = (f32[16,256]{1,0:T(8,128)S(1)}, f32[16,256]{1,0:T(8,128)S(1)}, f32[16,256]{1,0:T(8,128)S(1)}, f32[16,256]{1,0:T(8,128)S(1)}) custom-call(s32[2]{0:T(128)S(1)} %pad_add_fusion.pos, bf16[16,512]{1,0:T(8,128)(2,1)S(1)} %shard_map.155.refs_0_, bf16[16,512]{1,0:T(8,128)(2,1)S(1)} %collective-permute-done.29.refs_1_, ...), custom_call_target="tpu_custom_call" | custom-call | flops 134217728 | bytes 8585216 | tf_op jit(solution)/shard_map/pallas_call | solution.py:330
  140.6 3.2 %collective-permute-start.36 = (f32[16,256]{1,0:T(8,128)S(1)}, f32[16,256]{1,0:T(8,128)S(1)}, u32[]{:S(2)}, u32[]{:S(2)}) collective-permute-start(f32[16,256]{1,0:T(8,128)S(1)} %get-tuple-element.33), channel_id=1, source_target_pairs={{0,1},{1,2},{2,3},{3,0},{4,5},{5,6},{6,7},{7,4},{8,9},{9,10},{10,1... | collective-permute-start | bytes 49160 | tf_op jit(solution)/shard_map/ppermute | solution.py:348
  143.8 1.3 collective-permute-done.38
  145.9 2.2 %copy-done.18 = bf16[256,8192]{1,0:T(8,128)(2,1)S(1)} copy-done((bf16[256,8192]{1,0:T(8,128)(2,1)S(1)}, bf16[256,8192]{1,0:T(8,128)(2,1)}, u32[]{:S(2)}) %copy-start.18) | copy-done | bytes 4194328
  148.1 44.3 %shard_map.149 = bf16[256,8192]{1,0:T(8,128)(2,1)} custom-call(s32[16]{0:T(128)S(1)} %copy-done.17, s32[16]{0:T(128)S(1)} %copy-done.12, s32[2]{0:T(128)S(1)} %pad_add_fusion.pos, bf16[256,8192]{1,0:T(8,128)(2,1)S(1)} %copy-done.18, bf16[256,1024]{1,0:T(8,128)(2,1)S(1)} %copy-done.5, bf16[256,1024]{1,0:T(8,128)(2,1)S(1)} %collective-permute-done.refs_2_, ...), custom_call_target="tpu_custom_call" | custom-call | flops 17179869184 | bytes 12582912 | tf_op jit(solution)/shard_map/pallas_call | solution.py:330
  (82 shorter events, 13.2 us)
Async XLA Ops:
  0.6 14.9 %collective-permute-start = (bf16[256,1024]{1,0:T(8,128)(2,1)}, bf16[256,1024]{1,0:T(8,128)(2,1)S(1)}, u32[]{:S(2)}, u32[]{:S(2)}) collective-permute-start(bf16[256,1024]{1,0:T(8,128)(2,1)} %refs_4_.2), channel_id=1, source_target_pairs={{0,1},{1,2},{2,3},{4,5},{5,6},{6,7},{8,9},{9,10},{10,11},{12,13},{... | collective-permute-start | bytes 1572872 | tf_op jit(solution)/shard_map/ppermute | solution.py:385
  1.9 24.8 %collective-permute-start.3 = (bf16[256,1024]{1,0:T(8,128)(2,1)}, bf16[256,1024]{1,0:T(8,128)(2,1)S(1)}, u32[]{:S(2)}, u32[]{:S(2)}) collective-permute-start(bf16[256,1024]{1,0:T(8,128)(2,1)} %refs_5_.4), channel_id=1, source_target_pairs={{0,1},{1,2},{2,3},{4,5},{5,6},{6,7},{8,9},{9,10},{10,11},{12,13},{... | collective-permute-start | bytes 1572872 | tf_op jit(solution)/shard_map/ppermute | solution.py:386
  15.5 58.1 %collective-permute-start.1 = (bf16[256,1024]{1,0:T(8,128)(2,1)S(1)}, bf16[256,1024]{1,0:T(8,128)(2,1)S(1)}, u32[]{:S(2)}, u32[]{:S(2)}) collective-permute-start(bf16[256,1024]{1,0:T(8,128)(2,1)S(1)} %collective-permute-done.refs_2_), channel_id=1, source_target_pairs={{1,2},{2,3},{5,6},{6,7},{9,10},{10,11},{13,14},{14,15},{17,18},{18... | collective-permute-start | bytes 1572872 | tf_op jit(solution)/shard_map/ppermute | solution.py:385
  26.8 48.2 %collective-permute-start.4 = (bf16[256,1024]{1,0:T(8,128)(2,1)S(1)}, bf16[256,1024]{1,0:T(8,128)(2,1)S(1)}, u32[]{:S(2)}, u32[]{:S(2)}) collective-permute-start(bf16[256,1024]{1,0:T(8,128)(2,1)S(1)} %collective-permute-done.3.refs_6_), channel_id=1, source_target_pairs={{1,2},{2,3},{5,6},{6,7},{9,10},{10,11},{13,14},{14,15},{17,18},{18... | collective-permute-start | bytes 1572872 | tf_op jit(solution)/shard_map/ppermute | solution.py:386
  31.0 18.9 %collective-permute-start.6 = (bf16[4,2048]{1,0:T(4,128)(2,1)S(1)}, bf16[4,2048]{1,0:T(4,128)(2,1)S(1)}, u32[]{:S(2)}, u32[]{:S(2)}) collective-permute-start(bf16[4,2048]{1,0:T(4,128)(2,1)S(1)} %shard_map.150.refs_0_.refs_4_), channel_id=1, source_target_pairs={{0,1},{1,2},{2,3},{3,0},{4,5},{5,6},{6,7},{7,4},{8,9},{9,10},{10,1... | collective-permute-start | bytes 49160 | tf_op jit(solution)/shard_map/ppermute | solution.py:348
  31.1 19.1 %collective-permute-start.7 = (bf16[4,2048]{1,0:T(4,128)(2,1)S(1)}, bf16[4,2048]{1,0:T(4,128)(2,1)S(1)}, u32[]{:S(2)}, u32[]{:S(2)}) collective-permute-start(bf16[4,2048]{1,0:T(4,128)(2,1)S(1)} %shard_map.150.refs_0_.refs_4_), channel_id=1, source_target_pairs={{0,2},{1,3},{2,0},{3,1},{4,6},{5,7},{6,4},{7,5},{8,10},{9,11},{10,... | collective-permute-start | bytes 49160 | tf_op jit(solution)/shard_map/ppermute | solution.py:348
  34.3 15.9 %collective-permute-start.8 = (bf16[4,2048]{1,0:T(4,128)(2,1)S(1)}, bf16[4,2048]{1,0:T(4,128)(2,1)S(1)}, u32[]{:S(2)}, u32[]{:S(2)}) collective-permute-start(bf16[4,2048]{1,0:T(4,128)(2,1)S(1)} %shard_map.150.refs_0_.refs_4_), channel_id=1, source_target_pairs={{0,3},{1,0},{2,1},{3,2},{4,7},{5,4},{6,5},{7,6},{8,11},{9,8},{10,9... | collective-permute-start | bytes 49160 | tf_op jit(solution)/shard_map/ppermute | solution.py:348
  56.2 4.6 %collective-permute-start.9 = (bf16[64,256]{1,0:T(8,128)(2,1)S(1)}, bf16[64,256]{1,0:T(8,128)(2,1)S(1)}, u32[]{:S(2)}, u32[]{:S(2)}) collective-permute-start(bf16[64,256]{1,0:T(8,128)(2,1)S(1)} %get-tuple-element.20), channel_id=1, source_target_pairs={{0,3},{1,0},{2,1},{3,2},{4,7},{5,4},{6,5},{7,6},{8,11},{9,8},{10,9... | collective-permute-start | bytes 98312 | tf_op jit(solution)/shard_map/ppermute | solution.py:348
  56.5 4.3 %collective-permute-start.10 = (bf16[64,256]{1,0:T(8,128)(2,1)S(1)}, bf16[64,256]{1,0:T(8,128)(2,1)S(1)}, u32[]{:S(2)}, u32[]{:S(2)}) collective-permute-start(bf16[64,256]{1,0:T(8,128)(2,1)S(1)} %get-tuple-element.21), channel_id=1, source_target_pairs={{0,2},{1,3},{2,0},{3,1},{4,6},{5,7},{6,4},{7,5},{8,10},{9,11},{10,... | collective-permute-start | bytes 98312 | tf_op jit(solution)/shard_map/ppermute | solution.py:348
  56.5 4.7 %collective-permute-start.11 = (bf16[64,256]{1,0:T(8,128)(2,1)S(1)}, bf16[64,256]{1,0:T(8,128)(2,1)S(1)}, u32[]{:S(2)}, u32[]{:S(2)}) collective-permute-start(bf16[64,256]{1,0:T(8,128)(2,1)S(1)} %get-tuple-element.22), channel_id=1, source_target_pairs={{0,1},{1,2},{2,3},{3,0},{4,5},{5,6},{6,7},{7,4},{8,9},{9,10},{10,1... | collective-permute-start | bytes 98312 | tf_op jit(solution)/shard_map/ppermute | solution.py:348
  63.5 5.1 %collective-permute-start.12 = (bf16[4,2048]{1,0:T(4,128)(2,1)S(1)}, bf16[4,2048]{1,0:T(4,128)(2,1)S(1)}, u32[]{:S(2)}, u32[]{:S(2)}) collective-permute-start(bf16[4,2048]{1,0:T(4,128)(2,1)S(1)} %shard_map.152.refs_0_), channel_id=1, source_target_pairs={{0,4},{4,8},{8,12},{12,16},{16,20},{20,24},{24,28},{28,0},{1,5},{5... | collective-permute-start | bytes 49160 | tf_op jit(solution)/shard_map/ppermute | solution.py:348
  67.0 2.6 %collective-permute-start.13 = (bf16[4,2048]{1,0:T(4,128)(2,1)S(1)}, bf16[4,2048]{1,0:T(4,128)(2,1)S(1)}, u32[]{:S(2)}, u32[]{:S(2)}) collective-permute-start(bf16[4,2048]{1,0:T(4,128)(2,1)S(1)} %shard_map.152.refs_0_), channel_id=1, source_target_pairs={{0,8},{4,12},{8,16},{12,20},{16,24},{20,28},{24,0},{28,4},{1,9},{5... | collective-permute-start | bytes 49160 | tf_op jit(solution)/shard_map/ppermute | solution.py:348
  68.3 3.5 %collective-permute-start.14 = (bf16[4,2048]{1,0:T(4,128)(2,1)S(1)}, bf16[4,2048]{1,0:T(4,128)(2,1)S(1)}, u32[]{:S(2)}, u32[]{:S(2)}) collective-permute-start(bf16[4,2048]{1,0:T(4,128)(2,1)S(1)} %shard_map.152.refs_0_), channel_id=1, source_target_pairs={{0,12},{4,16},{8,20},{12,24},{16,28},{20,0},{24,4},{28,8},{1,13},{... | collective-permute-start | bytes 49160 | tf_op jit(solution)/shard_map/ppermute | solution.py:348
  68.6 4.2 %collective-permute-start.15 = (bf16[4,2048]{1,0:T(4,128)(2,1)S(1)}, bf16[4,2048]{1,0:T(4,128)(2,1)S(1)}, u32[]{:S(2)}, u32[]{:S(2)}) collective-permute-start(bf16[4,2048]{1,0:T(4,128)(2,1)S(1)} %shard_map.152.refs_0_), channel_id=1, source_target_pairs={{0,16},{4,20},{8,24},{12,28},{16,0},{20,4},{24,8},{28,12},{1,17},{... | collective-permute-start | bytes 49160 | tf_op jit(solution)/shard_map/ppermute | solution.py:348
  69.7 6.7 %collective-permute-start.16 = (bf16[4,2048]{1,0:T(4,128)(2,1)S(1)}, bf16[4,2048]{1,0:T(4,128)(2,1)S(1)}, u32[]{:S(2)}, u32[]{:S(2)}) collective-permute-start(bf16[4,2048]{1,0:T(4,128)(2,1)S(1)} %shard_map.152.refs_0_), channel_id=1, source_target_pairs={{0,20},{4,24},{8,28},{12,0},{16,4},{20,8},{24,12},{28,16},{1,21},{... | collective-permute-start | bytes 49160 | tf_op jit(solution)/shard_map/ppermute | solution.py:348
  71.8 4.6 %collective-permute-start.17 = (bf16[4,2048]{1,0:T(4,128)(2,1)S(1)}, bf16[4,2048]{1,0:T(4,128)(2,1)S(1)}, u32[]{:S(2)}, u32[]{:S(2)}) collective-permute-start(bf16[4,2048]{1,0:T(4,128)(2,1)S(1)} %shard_map.152.refs_0_), channel_id=1, source_target_pairs={{0,24},{4,28},{8,0},{12,4},{16,8},{20,12},{24,16},{28,20},{1,25},{... | collective-permute-start | bytes 49160 | tf_op jit(solution)/shard_map/ppermute | solution.py:348
  72.8 4.1 %collective-permute-start.18 = (bf16[4,2048]{1,0:T(4,128)(2,1)S(1)}, bf16[4,2048]{1,0:T(4,128)(2,1)S(1)}, u32[]{:S(2)}, u32[]{:S(2)}) collective-permute-start(bf16[4,2048]{1,0:T(4,128)(2,1)S(1)} %shard_map.152.refs_0_), channel_id=1, source_target_pairs={{0,28},{4,0},{8,4},{12,8},{16,12},{20,16},{24,20},{28,24},{1,29},{... | collective-permute-start | bytes 49160 | tf_op jit(solution)/shard_map/ppermute | solution.py:348
  73.7 72.2 %collective-permute-start.2 = (bf16[256,1024]{1,0:T(8,128)(2,1)S(1)}, bf16[256,1024]{1,0:T(8,128)(2,1)}, u32[]{:S(2)}, u32[]{:S(2)}) collective-permute-start(bf16[256,1024]{1,0:T(8,128)(2,1)S(1)} %collective-permute-done.1.refs_3_), channel_id=1, source_target_pairs={{2,3},{6,7},{10,11},{14,15},{18,19},{22,23},{26,27},{30,31}} | collective-permute-start | bytes 1572872 | tf_op jit(solution)/shard_map/ppermute | solution.py:385
  75.0 70.9 %collective-permute-start.5 = (bf16[256,1024]{1,0:T(8,128)(2,1)S(1)}, bf16[256,1024]{1,0:T(8,128)(2,1)}, u32[]{:S(2)}, u32[]{:S(2)}) collective-permute-start(bf16[256,1024]{1,0:T(8,128)(2,1)S(1)} %collective-permute-done.4.refs_7_), channel_id=1, source_target_pairs={{2,3},{6,7},{10,11},{14,15},{18,19},{22,23},{26,27},{30,31}} | collective-permute-start | bytes 1572872 | tf_op jit(solution)/shard_map/ppermute | solution.py:386
  76.9 2.2 %copy-start.3 = (bf16[2048,1024]{1,0:T(8,128)(2,1)S(1)}, bf16[2048,1024]{1,0:T(8,128)(2,1)}, u32[]{:S(2)}) copy-start(bf16[2048,1024]{1,0:T(8,128)(2,1)} %refs_8_.2) | copy-start | bytes 12582916
  80.8 21.0 %collective-permute-start.19 = (bf16[16,1024]{1,0:T(8,128)(2,1)S(1)}, bf16[16,1024]{1,0:T(8,128)(2,1)S(1)}, u32[]{:S(2)}, u32[]{:S(2)}) collective-permute-start(bf16[16,1024]{1,0:T(8,128)(2,1)S(1)} %shard_map.153.refs_0_), channel_id=1, source_target_pairs={{0,1},{1,2},{2,3},{3,0},{4,5},{5,6},{6,7},{7,4},{8,9},{9,10},{10,1... | collective-permute-start | bytes 98312 | tf_op jit(solution)/shard_map/ppermute | solution.py:348
  83.8 18.0 %collective-permute-start.20 = (bf16[16,1024]{1,0:T(8,128)(2,1)S(1)}, bf16[16,1024]{1,0:T(8,128)(2,1)S(1)}, u32[]{:S(2)}, u32[]{:S(2)}) collective-permute-start(bf16[16,1024]{1,0:T(8,128)(2,1)S(1)} %shard_map.153.refs_0_), channel_id=1, source_target_pairs={{0,2},{1,3},{2,0},{3,1},{4,6},{5,7},{6,4},{7,5},{8,10},{9,11},{10,... | collective-permute-start | bytes 98312 | tf_op jit(solution)/shard_map/ppermute | solution.py:348
  85.2 16.6 %collective-permute-start.21 = (bf16[16,1024]{1,0:T(8,128)(2,1)S(1)}, bf16[16,1024]{1,0:T(8,128)(2,1)S(1)}, u32[]{:S(2)}, u32[]{:S(2)}) collective-permute-start(bf16[16,1024]{1,0:T(8,128)(2,1)S(1)} %shard_map.153.refs_0_), channel_id=1, source_target_pairs={{0,3},{1,0},{2,1},{3,2},{4,7},{5,4},{6,5},{7,6},{8,11},{9,8},{10,9... | collective-permute-start | bytes 98312 | tf_op jit(solution)/shard_map/ppermute | solution.py:348
  101.8 3.4 %copy-start = (bf16[1024,4096]{1,0:T(8,128)(2,1)S(1)}, bf16[1024,4096]{1,0:T(8,128)(2,1)}, u32[]{:S(2)}) copy-start(bf16[1024,4096]{1,0:T(8,128)(2,1)} %refs_6_.3) | copy-start | bytes 25165828
  105.2 3.4 %copy-start.1 = (bf16[1024,4096]{1,0:T(8,128)(2,1)S(1)}, bf16[1024,4096]{1,0:T(8,128)(2,1)}, u32[]{:S(2)}) copy-start(bf16[1024,4096]{1,0:T(8,128)(2,1)} %refs_7_.1) | copy-start | bytes 25165828
  109.3 28.6 %copy-start.2 = (bf16[4096,1024]{1,0:T(8,128)(2,1)S(1)}, bf16[4096,1024]{1,0:T(8,128)(2,1)}, u32[]{:S(2)}) copy-start(bf16[4096,1024]{1,0:T(8,128)(2,1)} %refs_8_.3) | copy-start | bytes 25165828
  114.4 31.4 %copy-start.5 = (bf16[256,1024]{1,0:T(8,128)(2,1)S(1)}, bf16[256,1024]{1,0:T(8,128)(2,1)}, u32[]{:S(2)}) copy-start(bf16[256,1024]{1,0:T(8,128)(2,1)} %refs_4_.2) | copy-start | bytes 1572868
  114.4 31.4 %copy-start.7 = (bf16[256,1024]{1,0:T(8,128)(2,1)S(1)}, bf16[256,1024]{1,0:T(8,128)(2,1)}, u32[]{:S(2)}) copy-start(bf16[256,1024]{1,0:T(8,128)(2,1)} %refs_5_.4) | copy-start | bytes 1572868
  114.5 31.4 %copy-start.12 = (s32[16]{0:T(128)S(1)}, s32[16]{0:T(128)}, u32[]{:S(2)}) copy-start(s32[16]{0:T(128)} %groups.7) | copy-start | bytes 196
  114.5 31.4 %copy-start.17 = (s32[16]{0:T(128)S(1)}, s32[16]{0:T(128)}, u32[]{:S(2)}) copy-start(s32[16]{0:T(128)} %lengths.7) | copy-start | bytes 196
  114.5 4.1 %collective-permute-start.22 = (bf16[16,1152]{1,0:T(8,128)(2,1)S(1)}, bf16[16,1152]{1,0:T(8,128)(2,1)S(1)}, u32[]{:S(2)}, u32[]{:S(2)}) collective-permute-start(bf16[16,1152]{1,0:T(8,128)(2,1)S(1)} %get-tuple-element.25), channel_id=1, source_target_pairs={{0,4},{4,8},{8,12},{12,16},{16,20},{20,24},{24,28},{28,0},{1,5},{5... | collective-permute-start | bytes 110600 | tf_op jit(solution)/shard_map/ppermute | solution.py:348
  117.1 3.1 %collective-permute-start.23 = (bf16[16,1152]{1,0:T(8,128)(2,1)S(1)}, bf16[16,1152]{1,0:T(8,128)(2,1)S(1)}, u32[]{:S(2)}, u32[]{:S(2)}) collective-permute-start(bf16[16,1152]{1,0:T(8,128)(2,1)S(1)} %get-tuple-element.26), channel_id=1, source_target_pairs={{0,8},{4,12},{8,16},{12,20},{16,24},{20,28},{24,0},{28,4},{1,9},{5... | collective-permute-start | bytes 110600 | tf_op jit(solution)/shard_map/ppermute | solution.py:348
  117.4 4.8 %collective-permute-start.24 = (bf16[16,1152]{1,0:T(8,128)(2,1)S(1)}, bf16[16,1152]{1,0:T(8,128)(2,1)S(1)}, u32[]{:S(2)}, u32[]{:S(2)}) collective-permute-start(bf16[16,1152]{1,0:T(8,128)(2,1)S(1)} %get-tuple-element.27), channel_id=1, source_target_pairs={{0,12},{4,16},{8,20},{12,24},{16,28},{20,0},{24,4},{28,8},{1,13},{... | collective-permute-start | bytes 110600 | tf_op jit(solution)/shard_map/ppermute | solution.py:348
  118.6 4.2 %collective-permute-start.25 = (bf16[16,1152]{1,0:T(8,128)(2,1)S(1)}, bf16[16,1152]{1,0:T(8,128)(2,1)S(1)}, u32[]{:S(2)}, u32[]{:S(2)}) collective-permute-start(bf16[16,1152]{1,0:T(8,128)(2,1)S(1)} %get-tuple-element.28), channel_id=1, source_target_pairs={{0,16},{4,20},{8,24},{12,28},{16,0},{20,4},{24,8},{28,12},{1,17},{... | collective-permute-start | bytes 110600 | tf_op jit(solution)/shard_map/ppermute | solution.py:348
  120.2 3.7 %collective-permute-start.26 = (bf16[16,1152]{1,0:T(8,128)(2,1)S(1)}, bf16[16,1152]{1,0:T(8,128)(2,1)S(1)}, u32[]{:S(2)}, u32[]{:S(2)}) collective-permute-start(bf16[16,1152]{1,0:T(8,128)(2,1)S(1)} %get-tuple-element.29), channel_id=1, source_target_pairs={{0,20},{4,24},{8,28},{12,0},{16,4},{20,8},{24,12},{28,16},{1,21},{... | collective-permute-start | bytes 110600 | tf_op jit(solution)/shard_map/ppermute | solution.py:348
  122.2 4.3 %collective-permute-start.27 = (bf16[16,1152]{1,0:T(8,128)(2,1)S(1)}, bf16[16,1152]{1,0:T(8,128)(2,1)S(1)}, u32[]{:S(2)}, u32[]{:S(2)}) collective-permute-start(bf16[16,1152]{1,0:T(8,128)(2,1)S(1)} %get-tuple-element.30), channel_id=1, source_target_pairs={{0,24},{4,28},{8,0},{12,4},{16,8},{20,12},{24,16},{28,20},{1,25},{... | collective-permute-start | bytes 110600 | tf_op jit(solution)/shard_map/ppermute | solution.py:348
  122.8 4.3 %collective-permute-start.28 = (bf16[16,1152]{1,0:T(8,128)(2,1)S(1)}, bf16[16,1152]{1,0:T(8,128)(2,1)S(1)}, u32[]{:S(2)}, u32[]{:S(2)}) collective-permute-start(bf16[16,1152]{1,0:T(8,128)(2,1)S(1)} %get-tuple-element.31), channel_id=1, source_target_pairs={{0,28},{4,0},{8,4},{12,8},{16,12},{20,16},{24,20},{28,24},{1,29},{... | collective-permute-start | bytes 110600 | tf_op jit(solution)/shard_map/ppermute | solution.py:348
  127.3 2.5 %collective-permute-start.29 = (bf16[16,512]{1,0:T(8,128)(2,1)S(1)}, bf16[16,512]{1,0:T(8,128)(2,1)S(1)}, u32[]{:S(2)}, u32[]{:S(2)}) collective-permute-start(bf16[16,512]{1,0:T(8,128)(2,1)S(1)} %shard_map.155.refs_0_), channel_id=1, source_target_pairs={{0,4},{4,8},{8,12},{12,16},{16,20},{20,24},{24,28},{28,0},{1,5},{5... | collective-permute-start | bytes 49160 | tf_op jit(solution)/shard_map/ppermute | solution.py:348
  127.7 2.7 %collective-permute-start.30 = (bf16[16,512]{1,0:T(8,128)(2,1)S(1)}, bf16[16,512]{1,0:T(8,128)(2,1)S(1)}, u32[]{:S(2)}, u32[]{:S(2)}) collective-permute-start(bf16[16,512]{1,0:T(8,128)(2,1)S(1)} %shard_map.155.refs_0_), channel_id=1, source_target_pairs={{0,8},{4,12},{8,16},{12,20},{16,24},{20,28},{24,0},{28,4},{1,9},{5... | collective-permute-start | bytes 49160 | tf_op jit(solution)/shard_map/ppermute | solution.py:348
  128.3 4.7 %collective-permute-start.31 = (bf16[16,512]{1,0:T(8,128)(2,1)S(1)}, bf16[16,512]{1,0:T(8,128)(2,1)S(1)}, u32[]{:S(2)}, u32[]{:S(2)}) collective-permute-start(bf16[16,512]{1,0:T(8,128)(2,1)S(1)} %shard_map.155.refs_0_), channel_id=1, source_target_pairs={{0,12},{4,16},{8,20},{12,24},{16,28},{20,0},{24,4},{28,8},{1,13},{... | collective-permute-start | bytes 49160 | tf_op jit(solution)/shard_map/ppermute | solution.py:348
  129.8 4.1 %collective-permute-start.32 = (bf16[16,512]{1,0:T(8,128)(2,1)S(1)}, bf16[16,512]{1,0:T(8,128)(2,1)S(1)}, u32[]{:S(2)}, u32[]{:S(2)}) collective-permute-start(bf16[16,512]{1,0:T(8,128)(2,1)S(1)} %shard_map.155.refs_0_), channel_id=1, source_target_pairs={{0,16},{4,20},{8,24},{12,28},{16,0},{20,4},{24,8},{28,12},{1,17},{... | collective-permute-start | bytes 49160 | tf_op jit(solution)/shard_map/ppermute | solution.py:348
  130.3 3.7 %collective-permute-start.33 = (bf16[16,512]{1,0:T(8,128)(2,1)S(1)}, bf16[16,512]{1,0:T(8,128)(2,1)S(1)}, u32[]{:S(2)}, u32[]{:S(2)}) collective-permute-start(bf16[16,512]{1,0:T(8,128)(2,1)S(1)} %shard_map.155.refs_0_), channel_id=1, source_target_pairs={{0,20},{4,24},{8,28},{12,0},{16,4},{20,8},{24,12},{28,16},{1,21},{... | collective-permute-start | bytes 49160 | tf_op jit(solution)/shard_map/ppermute | solution.py:348
  132.9 3.5 %collective-permute-start.34 = (bf16[16,512]{1,0:T(8,128)(2,1)S(1)}, bf16[16,512]{1,0:T(8,128)(2,1)S(1)}, u32[]{:S(2)}, u32[]{:S(2)}) collective-permute-start(bf16[16,512]{1,0:T(8,128)(2,1)S(1)} %shard_map.155.refs_0_), channel_id=1, source_target_pairs={{0,24},{4,28},{8,0},{12,4},{16,8},{20,12},{24,16},{28,20},{1,25},{... | collective-permute-start | bytes 49160 | tf_op jit(solution)/shard_map/ppermute | solution.py:348
  133.8 4.1 %collective-permute-start.35 = (bf16[16,512]{1,0:T(8,128)(2,1)S(1)}, bf16[16,512]{1,0:T(8,128)(2,1)S(1)}, u32[]{:S(2)}, u32[]{:S(2)}) collective-permute-start(bf16[16,512]{1,0:T(8,128)(2,1)S(1)} %shard_map.155.refs_0_), channel_id=1, source_target_pairs={{0,28},{4,0},{8,4},{12,8},{16,12},{20,16},{24,20},{28,24},{1,29},{... | collective-permute-start | bytes 49160 | tf_op jit(solution)/shard_map/ppermute | solution.py:348
  140.5 4.6 %collective-permute-start.38 = (f32[16,256]{1,0:T(8,128)S(1)}, f32[16,256]{1,0:T(8,128)S(1)}, u32[]{:S(2)}, u32[]{:S(2)}) collective-permute-start(f32[16,256]{1,0:T(8,128)S(1)} %get-tuple-element.35), channel_id=1, source_target_pairs={{0,3},{1,0},{2,1},{3,2},{4,7},{5,4},{6,5},{7,6},{8,11},{9,8},{10,9... | collective-permute-start | bytes 49160 | tf_op jit(solution)/shard_map/ppermute | solution.py:348
  140.5 4.5 %collective-permute-start.37 = (f32[16,256]{1,0:T(8,128)S(1)}, f32[16,256]{1,0:T(8,128)S(1)}, u32[]{:S(2)}, u32[]{:S(2)}) collective-permute-start(f32[16,256]{1,0:T(8,128)S(1)} %get-tuple-element.34), channel_id=1, source_target_pairs={{0,2},{1,3},{2,0},{3,1},{4,6},{5,7},{6,4},{7,5},{8,10},{9,11},{10,... | collective-permute-start | bytes 49160 | tf_op jit(solution)/shard_map/ppermute | solution.py:348
  140.6 4.6 %collective-permute-start.36 = (f32[16,256]{1,0:T(8,128)S(1)}, f32[16,256]{1,0:T(8,128)S(1)}, u32[]{:S(2)}, u32[]{:S(2)}) collective-permute-start(f32[16,256]{1,0:T(8,128)S(1)} %get-tuple-element.33), channel_id=1, source_target_pairs={{0,1},{1,2},{2,3},{3,0},{4,5},{5,6},{6,7},{7,4},{8,9},{9,10},{10,1... | collective-permute-start | bytes 49160 | tf_op jit(solution)/shard_map/ppermute | solution.py:348
  145.9 2.2 %copy-start.18 = (bf16[256,8192]{1,0:T(8,128)(2,1)S(1)}, bf16[256,8192]{1,0:T(8,128)(2,1)}, u32[]{:S(2)}) copy-start(bf16[256,8192]{1,0:T(8,128)(2,1)} %refs_0_.1) | copy-start | bytes 12582916
  (10 other events, 7.7 us)

commit v2 on v1

v2 whole, which is shorter than its diff:
```python
import functools
import math

import jax
import jax.numpy as jnp
from jax import lax
from jax.experimental import pallas as pl
from jax.experimental.pallas import tpu as pltpu
from jax.sharding import PartitionSpec as P

HD = 128
Q_PER_KV = 8
MAX_IN_GROUP = 3
SLOTS_R = 4
NEGATIVE = -1e30
LOG2E = 1.4426950408889634
MIB = 1 << 20
STREAM = 57

F32 = jnp.float32
BF16 = jnp.bfloat16


def dot(a, b):
    return jnp.dot(a, b, preferred_element_type=F32)


def dot_t(a, b):
    return lax.dot_general(a, b, (((1,), (1,)), ((), ())), preferred_element_type=F32)


def plan(facts):
    group = facts[0]
    reqs = (facts.shape[0] - 2) // 2
    ids = [jnp.int32(-1)] * MAX_IN_GROUP
    first = [jnp.int32(0)] * MAX_IN_GROUP
    end = [jnp.int32(0)] * MAX_IN_GROUP
    count = jnp.int32(0)
    used = jnp.int32(0)
    for r in range(reqs):
        mine = facts[2 + r] == group
        length = facts[2 + reqs + r]
        for k in range(MAX_IN_GROUP):
            here = mine & (count == k)
            ids[k] = jnp.where(here, r, ids[k])
            first[k] = jnp.where(here, used, first[k])
            end[k] = jnp.where(here, used + length, end[k])
        count = count + jnp.where(mine, 1, 0)
        used = used + jnp.where(mine, length, 0)
    return ids, first, end


def pick_rows(ids, rows, columns):
    row = lax.broadcasted_iota(jnp.int32, (rows, columns), 0)
    column = lax.broadcasted_iota(jnp.int32, (rows, columns), 1)
    target = jnp.full((rows, columns), -1, jnp.int32)
    for k in range(MAX_IN_GROUP):
        target = jnp.where(row == k, ids[k], target)
    return jnp.where(column == target, 1.0, 0.0).astype(BF16)


def split3(x):
    hi = x.astype(BF16)
    rest = x - hi.astype(F32)
    mid = rest.astype(BF16)
    low = (rest - mid.astype(F32)).astype(BF16)
    return hi, mid, low


def select_kernel(facts, query_ref, out_ref):
    ids, _, _ = plan(facts)
    pick = pick_rows(ids, 8, query_ref.shape[0])
    out_ref[...] = dot(pick, query_ref[...])[:SLOTS_R].astype(BF16)


def partial_kernel(n, facts, *refs):
    queries, (key_ref, value_ref), outs = refs[:n], refs[n : n + 2], refs[n + 2 :]
    _, first, end = plan(facts)
    tokens = key_ref.shape[0]
    kv_per = queries[0].shape[1] // (HD * Q_PER_KV)
    rows = Q_PER_KV * SLOTS_R
    slot = facts[1] * tokens + lax.broadcasted_iota(jnp.int32, (rows, tokens), 1)
    rank = lax.broadcasted_iota(jnp.int32, (rows, tokens), 0) & (SLOTS_R - 1)
    low = jnp.zeros((rows, tokens), jnp.int32)
    high = jnp.zeros((rows, tokens), jnp.int32)
    for k in range(MAX_IN_GROUP):
        low = jnp.where(rank == k, first[k], low)
        high = jnp.where(rank == k, end[k], high)
    allowed = (slot >= low) & (slot < high)
    lane = lax.broadcasted_iota(jnp.int32, (rows, HD), 1)
    scale = 1.0 / math.sqrt(HD)
    for t in range(n):
        shard = lax.rem(facts[1] - t + n, n)
        query = queries[t][...].astype(F32)
        for i in range(kv_per):
            columns = pl.ds(pl.multiple_of((shard * kv_per + i) * HD, HD), HD)
            keys = key_ref[:, columns]
            values = value_ref[:, columns]
            heads = [query[:, (i * Q_PER_KV + h) * HD :][:, :HD] for h in range(Q_PER_KV)]
            stacked = jnp.concatenate(heads, axis=0).astype(BF16)
            scores = jnp.where(allowed, dot_t(stacked, keys) * scale, NEGATIVE)
            top = jnp.max(scores, axis=1, keepdims=True)
            weights = jnp.where(allowed, jnp.exp(scores - top), 0.0)
            total = jnp.sum(weights, axis=1, keepdims=True)
            some = total > 0.0
            mixed = dot(weights.astype(BF16), values) / jnp.where(some, total, 1.0)
            level = jnp.where(some, top + jnp.log(jnp.where(some, total, 1.0)), NEGATIVE)
            hi, mid, rest = split3(jnp.broadcast_to(level, (rows, HD)))
            stats = jnp.where(
                lane < 32, hi.astype(F32), jnp.where(lane < 64, mid.astype(F32), rest.astype(F32))
            )
            outs[t][i * rows : (i + 1) * rows, :] = jnp.concatenate([mixed, stats], axis=1).astype(
                BF16
            )


def combine_kernel(n, count, facts, *refs):
    parts, (query_ref, key_ref, value_ref, out_ref) = refs[:n], refs[n:]
    ids, _, _ = plan(facts)
    heads = query_ref.shape[1] // HD
    pick = pick_rows(ids, 8, key_ref.shape[0])
    keys = dot(pick, key_ref[...])[:SLOTS_R]
    values = dot(pick, value_ref[...])[:SLOTS_R]
    query = query_ref[...].astype(F32)

    def by_head(array, group):
        return jnp.concatenate(
            [array[:, (h // group) * HD :][:, :HD] for h in range(heads)], axis=0
        )

    own_score = jnp.sum(
        by_head(query, 1) * by_head(keys, Q_PER_KV), axis=1, keepdims=True
    ) * (1.0 / math.sqrt(HD))
    own_value = by_head(values, Q_PER_KV)
    mixes = []
    levels = []
    top = own_score
    for t in range(n):
        part = parts[t][...].astype(F32)
        stats = part[:, HD:]
        level = stats[:, 0:1] + stats[:, 32:33] + stats[:, 64:65]
        mixes.append(part[:, :HD])
        levels.append(level)
        top = jnp.maximum(top, level)
    own_weight = jnp.exp(own_score - top)
    total = own_weight
    mixed = own_weight.astype(BF16).astype(F32) * own_value
    for t in range(n):
        weight = jnp.exp(levels[t] - top)
        total = total + weight
        mixed = mixed + weight * mixes[t]
    result = mixed / total
    for h in range(heads):
        head = result[h * SLOTS_R : (h + 1) * SLOTS_R].astype(BF16)
        for g in range(count):
            out_ref[g, :, h * HD : (h + 1) * HD] = head


def project_kernel(count, pick_ref, parts_ref, weight_ref, out_ref, att_ref, sum_ref):
    step = pl.program_id(0)
    depth = weight_ref.shape[0]

    @pl.when(step == 0)
    def _():
        stacked = jnp.concatenate([parts_ref[g].astype(F32) for g in range(count)], axis=0)
        att = dot(pick_ref[...], stacked.astype(BF16)).astype(BF16)
        for j in range(att_ref.shape[0]):
            att_ref[j] = att[:, j * depth : (j + 1) * depth]
        sum_ref[...] = jnp.zeros_like(sum_ref)

    sum_ref[...] += dot(att_ref[step], weight_ref[...])

    @pl.when(step == pl.num_programs(0) - 1)
    def _():
        out_ref[...] = sum_ref[...].astype(out_ref.dtype)


def gate_up_kernel(n, count, *refs):
    parts = refs[:n]
    hidden_ref, gain_ref, gate_ref, up_ref, resid_ref, send_ref, scaled_ref, stats_ref = refs[n:]
    step = pl.program_id(0)
    width = gate_ref.shape[1]

    @pl.when(step == 0)
    def _():
        resid = parts[0][...].astype(F32)
        for part in parts[1:]:
            resid = resid + part[...].astype(F32)
        resid = resid + hidden_ref[...].astype(F32)
        resid_ref[...] = resid
        scaled_ref[...] = (resid * gain_ref[...].astype(F32)).astype(BF16)
        squares = jnp.sum(resid * resid, axis=1, keepdims=True)
        rows = resid.shape[0]
        hi, mid, low = split3(jnp.broadcast_to(squares, (rows, HD)))
        lane = lax.broadcasted_iota(jnp.int32, (rows, HD), 1)
        stats_ref[...] = jnp.where(
            lane < 32, hi.astype(F32), jnp.where(lane < 64, mid.astype(F32), low.astype(F32))
        ).astype(BF16)

    scaled = scaled_ref[...]
    send_ref[step, :, :width] = dot(scaled, gate_ref[...]).astype(BF16)
    send_ref[step, :, width : 2 * width] = dot(scaled, up_ref[...]).astype(BF16)
    send_ref[step, :, 2 * width :] = stats_ref[...]


def hidden_kernel(count, features, parts_ref, out_ref):
    width = out_ref.shape[2]
    total = parts_ref[0].astype(F32)
    for g in range(1, count):
        total = total + parts_ref[g].astype(F32)
    stats = total[:, 2 * width :]
    squares = stats[:, 0:1] + stats[:, 32:33] + stats[:, 64:65]
    inverse = lax.rsqrt(squares / features + 1e-05)
    gate = total[:, :width] * inverse
    upper = total[:, width : 2 * width] * inverse
    hidden = (gate / (1.0 + jnp.exp(-gate)) * upper).astype(BF16)
    for g in range(count):
        out_ref[g] = hidden


def down_kernel(count, n, facts, parts_ref, weight_ref, *refs):
    sends, sum_ref = refs[:n], refs[n]
    step = pl.program_id(0)
    width = sends[0].shape[1]

    @pl.when(step == 0)
    def _():
        sum_ref[...] = jnp.zeros_like(sum_ref)

    sum_ref[...] += dot(parts_ref[step], weight_ref[...])

    for own in range(n):

        @pl.when((step == count - 1) & (facts[1] == own))
        def _():
            for t in range(n):
                target = (own + t) % n
                sends[t][...] = sum_ref[:, target * width : (target + 1) * width]


def row_facts(facts, tokens):
    _, first, end = plan(facts)
    row_first = facts[1] * tokens
    lowest = row_first + tokens
    for k in range(MAX_IN_GROUP):
        meets = (end[k] > row_first) & (first[k] < row_first + tokens)
        lowest = jnp.where(meets, jnp.minimum(lowest, first[k]), lowest)
    needed = facts[1] - lowest // tokens + 1
    return row_first, needed, first, end


def live_rows(row_first, first, end, tokens):
    row = row_first + lax.broadcasted_iota(jnp.int32, (tokens, HD), 0)
    live = row < 0
    for k in range(MAX_IN_GROUP):
        live = live | ((row >= first[k]) & (row < end[k]))
    return live


def store_bias(bias_ref, row_first, first, end, pieces):
    tokens = bias_ref.shape[0]
    row = row_first + lax.broadcasted_iota(jnp.int32, (tokens, tokens), 0)
    column = lax.broadcasted_iota(jnp.int32, (tokens, tokens), 1)
    low = jnp.full((tokens, tokens), 1 << 30, jnp.int32)
    for k in range(MAX_IN_GROUP):
        low = jnp.where((row >= first[k]) & (row < end[k]), first[k], low)
    for place, t in enumerate(pieces):
        slot = row_first - t * tokens + column
        bias_ref[:, place * tokens : (place + 1) * tokens] = jnp.where(
            (slot >= low) & (slot <= row), 0.0, NEGATIVE
        )


STACK = 4
EXP2 = LOG2E / math.sqrt(HD)


def inverse_of(x):
    guess = pl.reciprocal(x, approx=True)
    return guess * (2.0 - x * guess)


def stacked_heads(query_ref, at):
    return jnp.concatenate(
        [query_ref[:, h * HD : (h + 1) * HD] for h in range(at, at + STACK)], axis=0
    )


def near_kernel(m, facts, *refs):
    query_ref, keys, values = refs[0], refs[1 : 1 + m], refs[1 + m : 1 + 2 * m]
    out_ref, level_ref, bias_ref, value_ref = refs[1 + 2 * m :]
    tokens = query_ref.shape[0]
    row_first, needed, first, end = row_facts(facts, tokens)

    @pl.when(pl.program_id(0) == 0)
    def _():
        store_bias(bias_ref, row_first, first, end, range(m))
        value_ref[:, HD:] = jnp.ones((m * tokens, HD), BF16)

    @pl.when(needed == 0)
    def _():
        out_ref[...] = jnp.zeros_like(out_ref)

    def attend(count, masked, live):
        for t in range(count):
            value_ref[t * tokens : (t + 1) * tokens, :HD] = values[t][...]
        for at in range(0, Q_PER_KV, STACK):
            query = stacked_heads(query_ref, at)
            scores = []
            for t in range(count):
                score = dot_t(query, keys[t][...])
                if t in masked:
                    bias = bias_ref[:, t * tokens : (t + 1) * tokens]
                    score = (score.reshape(STACK, tokens, tokens) + bias[None]).reshape(
                        STACK * tokens, tokens
                    )
                scores.append(score)
            most = scores[0]
            for score in scores[1:]:
                most = jnp.maximum(most, score)
            top = jnp.max(most, axis=1, keepdims=True) * EXP2
            weights = jnp.concatenate(
                [jnp.exp2(score * EXP2 - top).astype(BF16) for score in scores], axis=1
            )
            mixed = dot(weights, value_ref[: count * tokens, :])
            result = mixed[:, :HD] * inverse_of(mixed[:, HD:])
            if count == m:
                level = top + jnp.log2(mixed[:, HD : HD + 1])
            for h in range(STACK):
                rows = slice(h * tokens, (h + 1) * tokens)
                head = result[rows]
                if live is not None:
                    head = jnp.where(live, head, 0.0)
                out_ref[:, (at + h) * HD : (at + h + 1) * HD] = head.astype(BF16)
                if count == m:
                    level_ref[:, at + h : at + h + 1] = level[rows]

    lone = needed < 0
    for k in range(MAX_IN_GROUP):
        lone = lone | (
            (first[k] <= row_first - (jnp.minimum(needed, m) - 1) * tokens)
            & (end[k] >= row_first + tokens)
        )
    before = 0
    for count in sorted({c for c in (1, 2, 3, m) if c <= m}):
        here = needed > before
        if count < m:
            here = here & (needed <= count)
        exact = here & ((needed >= count) if count == m else (needed == count)) & lone
        before = count

        @pl.when(exact)
        def _():
            attend(count, (0,), None)

        @pl.when(here & jnp.logical_not(exact))
        def _():
            attend(count, range(count), live_rows(row_first, first, end, tokens))


def far_kernel(n, facts, near_ref, level_ref, query_ref, key_ref, value_ref, out_ref, bias_ref, wide_ref):
    tokens = query_ref.shape[0]
    row_first, needed, first, end = row_facts(facts, tokens)

    @pl.when(needed < n)
    def _():
        out_ref[...] = near_ref[...]

    @pl.when(needed == n)
    def _():
        @pl.when(pl.program_id(0) == 0)
        def _():
            store_bias(bias_ref, row_first, first, end, (n - 1,))
            wide_ref[:, HD:] = jnp.ones((tokens, HD), BF16)

        wide_ref[:, :HD] = value_ref[...]
        live = live_rows(row_first, first, end, tokens)
        for at in range(0, Q_PER_KV, STACK):
            score = dot_t(stacked_heads(query_ref, at), key_ref[...])
            score = (score.reshape(STACK, tokens, tokens) + bias_ref[...][None]).reshape(
                STACK * tokens, tokens
            )
            level = jnp.concatenate(
                [level_ref[:, h : h + 1] for h in range(at, at + STACK)], axis=0
            )
            top = jnp.maximum(jnp.max(score, axis=1, keepdims=True) * EXP2, level)
            weights = jnp.exp2(score * EXP2 - top).astype(BF16)
            near_weight = jnp.exp2(level - top)
            mixed = dot(weights, wide_ref[...])
            inverse = inverse_of(mixed[:, HD:] + near_weight)
            for h in range(STACK):
                rows = slice(h * tokens, (h + 1) * tokens)
                columns = slice((at + h) * HD, (at + h + 1) * HD)
                near = near_ref[:, columns].astype(F32) * near_weight[rows]
                result = (mixed[rows, :HD] + near) * inverse[rows]
                out_ref[:, columns] = jnp.where(live, result, 0.0).astype(BF16)


def call(body, scalars, args, outs, *, grid=None, in_specs=None, out_specs=None, scratch=(), cost, vmem=6, aliases=None):
    whole = pl.BlockSpec(memory_space=pltpu.VMEM)
    if grid is None:
        grid = (1,)
    flops, exps = cost
    moved = sum(a.size * a.dtype.itemsize for a in args) + sum(
        o.size * o.dtype.itemsize for o in outs
    )
    return pl.pallas_call(
        body,
        out_shape=list(outs),
        grid_spec=pltpu.PrefetchScalarGridSpec(
            num_scalar_prefetch=len(scalars),
            grid=grid,
            in_specs=in_specs or [whole] * len(args),
            out_specs=out_specs or [whole] * len(outs),
            scratch_shapes=list(scratch),
        ),
        compiler_params=pltpu.CompilerParams(
            dimension_semantics=("arbitrary",) * len(grid), vmem_limit_bytes=vmem * MIB
        ),
        input_output_aliases=aliases or {},
        cost_estimate=pl.CostEstimate(flops=flops, bytes_accessed=moved, transcendentals=exps),
    )(*scalars, *args)


def shift(x, axis, count, t):
    return lax.ppermute(x, axis, [(i, (i + t) % count) for i in range(count)])


def shards(
    lengths,
    group_of,
    query_pre,
    key_pre,
    value_pre,
    query_new,
    key_new,
    value_new,
    hidden_new,
    out_weight,
    norm_gain,
    gate_weight,
    up_weight,
    down_weight,
):
    n = lax.axis_size("seq")
    count = lax.axis_size("grp")
    seq = lax.axis_index("seq").astype(jnp.int32)
    group = lax.axis_index("grp").astype(jnp.int32)
    tokens = query_pre.shape[0]
    reqs = query_new.shape[0]
    kv_heads = key_pre.shape[1] // HD
    shard_width = query_new.shape[1]
    shard_heads = shard_width // HD
    columns = out_weight.shape[1]
    shape = jax.ShapeDtypeStruct
    vmem = pl.BlockSpec(memory_space=pltpu.VMEM)
    facts = jnp.concatenate([jnp.stack([group, seq]), group_of, lengths])
    scalars = (facts,)

    def to_seq(x):
        return [x] + [shift(x, "seq", n, t) for t in range(1, n)]

    def to_grp(x):
        return lax.all_to_all(x, "grp", split_axis=0, concat_axis=0, tiled=True)

    def up(x, step, after):
        x, _ = lax.optimization_barrier((x, after))
        return lax.ppermute(x, "seq", [(i, i + 1) for i in range(step - 1, n - 1)])

    keys, values = [key_pre], [value_pre]

    (query,) = call(
        select_kernel,
        scalars,
        (query_new,),
        (shape((SLOTS_R, shard_width), BF16),),
        cost=(2 * 8 * reqs * shard_width, 0),
    )
    queries = to_seq(query)
    keys.append(up(keys[-1], 1, queries[1:]))
    rows = shard_heads * SLOTS_R
    partials = call(
        functools.partial(partial_kernel, n),
        scalars,
        (*queries, key_pre, value_pre),
        [shape((rows, 2 * HD), BF16)] * n,
        cost=(4 * n * rows * tokens * HD, n * rows * tokens),
    )
    partials = [partials[0]] + [shift(partials[t], "seq", n, n - t) for t in range(1, n)]
    values.append(up(values[-1], 1, partials[1:]))
    (att,) = call(
        functools.partial(combine_kernel, n, count),
        scalars,
        (*partials, query, key_new, value_new),
        (shape((count, SLOTS_R, shard_width), BF16),),
        cost=(8 * n * rows * HD, n * rows),
    )
    atts = to_grp(att)

    index = jnp.arange(reqs, dtype=jnp.int32)
    same = group_of[None, :] == group_of[:, None]
    rank = jnp.sum(jnp.where(same & (index[None, :] < index[:, None]), 1, 0), axis=1)
    place = group_of * SLOTS_R + rank
    pick = (place[:, None] == jnp.arange(count * SLOTS_R, dtype=jnp.int32)[None, :]).astype(BF16)
    steps = 4
    depth = shard_width // steps
    (proj,) = call(
        functools.partial(project_kernel, count),
        (),
        (pick, atts, out_weight),
        (shape((reqs, columns), BF16),),
        grid=(steps,),
        in_specs=[vmem, vmem, pl.BlockSpec((depth, columns), lambda j: (j, 0))],
        scratch=(pltpu.VMEM((steps, reqs, depth), BF16), pltpu.VMEM((reqs, columns), F32)),
        vmem=STREAM + 3,
        cost=(2 * reqs * shard_width * columns, 0),
    )
    projs = to_seq(proj)
    if n > 2:
        keys.append(up(keys[-1], 2, projs[1:]))
        values.append(up(values[-1], 2, projs[1:]))

    hidden_shard = gate_weight.shape[1]
    width = hidden_shard // count
    resid, terms = call(
        functools.partial(gate_up_kernel, n, count),
        (),
        (*projs, hidden_new, norm_gain.reshape(1, -1), gate_weight, up_weight),
        [shape((reqs, columns), F32), shape((count, reqs, 2 * width + HD), BF16)],
        grid=(count,),
        in_specs=[vmem] * (n + 2) + [pl.BlockSpec((columns, width), lambda j: (0, j))] * 2,
        scratch=(pltpu.VMEM((reqs, columns), BF16), pltpu.VMEM((reqs, HD), BF16)),
        vmem=STREAM,
        cost=(4 * reqs * columns * hidden_shard, 0),
    )
    (hidden,) = call(
        functools.partial(hidden_kernel, count, columns * count),
        (),
        (to_grp(terms),),
        (shape((count, reqs, width), BF16),),
        cost=(8 * count * reqs * width, reqs * width),
    )
    share = columns // n
    downs = call(
        functools.partial(down_kernel, count, n),
        scalars,
        (to_grp(hidden), down_weight),
        [shape((reqs, share), F32)] * n,
        grid=(count,),
        in_specs=[vmem, pl.BlockSpec((width, columns), lambda j, *_: (j, 0))],
        scratch=(pltpu.VMEM((reqs, columns), F32),),
        vmem=STREAM,
        cost=(2 * reqs * columns * hidden_shard, 0),
    )
    arrived = [shift(downs[t], "seq", n, t) for t in range(1, n)]
    total = lax.dynamic_slice_in_dim(resid, seq * share, share, 1) + downs[0]
    for part in arrived:
        total = total + part
    decode_hidden = total.astype(BF16)
    for step in range(len(keys), n):
        keys.append(up(keys[-1], step, arrived))
        values.append(up(values[-1], step, arrived))

    m = n - 1
    wide = Q_PER_KV * HD
    wide_block = pl.BlockSpec((tokens, wide), lambda h, *_: (0, h))
    head_block = pl.BlockSpec((tokens, HD), lambda h, *_: (0, h))
    level_block = pl.BlockSpec((None, tokens, Q_PER_KV), lambda h, *_: (h, 0, 0))
    near, levels = call(
        functools.partial(near_kernel, m),
        scalars,
        (query_pre, *keys[:m], *values[:m]),
        (shape(query_pre.shape, BF16), shape((kv_heads, tokens, Q_PER_KV), F32)),
        grid=(kv_heads,),
        in_specs=[wide_block] + [head_block] * (2 * m),
        out_specs=[wide_block, level_block],
        scratch=(
            pltpu.VMEM((tokens, m * tokens), F32),
            pltpu.VMEM((m * tokens, 2 * HD), BF16),
        ),
        cost=(8 * m * tokens * query_pre.size, m * tokens * query_pre.size // HD),
        vmem=STREAM + 3,
    )
    (prefill,) = call(
        functools.partial(far_kernel, n),
        scalars,
        (near, levels, query_pre, keys[m], values[m]),
        (shape(query_pre.shape, BF16),),
        grid=(kv_heads,),
        in_specs=[wide_block, level_block, wide_block, head_block, head_block],
        out_specs=[wide_block],
        scratch=(
            pltpu.VMEM((tokens, tokens), F32),
            pltpu.VMEM((tokens, 2 * HD), BF16),
        ),
        cost=(8 * tokens * query_pre.size, tokens * query_pre.size // HD),
        vmem=STREAM + 3,
        aliases={1: 0},
    )
    return (prefill, decode_hidden)


def solution(mesh):
    return jax.shard_map(
        shards,
        mesh=mesh,
        in_specs=(
            P(),
            P(),
            P(("grp", "seq"), None),
            P(("grp", "seq"), None),
            P(("grp", "seq"), None),
            P(None, "seq"),
            P(None, "seq"),
            P(None, "seq"),
            P(None, "grp"),
            P("seq", "grp"),
            P("grp"),
            P("grp", "seq"),
            P("grp", "seq"),
            P("seq", "grp"),
        ),
        out_specs=(P(("grp", "seq"), None), P(None, ("grp", "seq"))),
        check_vma=False,
    )
```

time: 194 us -> 154 us (0.79)
  the two profiles are of different devices: /device:TPU:31 before, /device:TPU:25 now
where the time goes in v2:
time: 154 us; the launch traced here: 152 us
  Pallas kernels  78.5 us (51%)
  starting transfers between devices  37.1 us (24%)
  waiting for transfers between devices  14.6 us (9%)
  blocking collectives  9.22 us (6%)
  local copies, waits for them, and re-layouts  7.15 us (5%)
  other arithmetic  4.33 us (3%)
    pallas_call x9, Pallas kernels, call(): pl.pallas_call(body, out_shape=list(outs), grid_spec=pltpu.PrefetchScalar...  78.5 us
    ppermute x12, starting transfers between devices, shift(): return lax.ppermute(x, axis, [(i, (i + t) % count) for i in range(count)])  16 us
    all_to_all x2, starting transfers between devices, to_grp(): return lax.all_to_all(x, 'grp', split_axis=0, concat_axis=0, tiled=True)  13.1 us
    all_to_all x1, blocking collectives, to_grp(): return lax.all_to_all(x, 'grp', split_axis=0, concat_axis=0, tiled=True)  9.22 us
    ppermute x6, starting transfers between devices, up(): return lax.ppermute(x, 'seq', [(i, i + 1) for i in range(step - 1, n - 1)])  7.9 us
    ppermute x12, waiting for transfers between devices, shift(): return lax.ppermute(x, axis, [(i, (i + t) % count) for i in range(count)])  7.44 us
    all_to_all x2, waiting for transfers between devices, to_grp(): return lax.all_to_all(x, 'grp', split_axis=0, concat_axis=0, tiled=True)  7.19 us
    unnamed x34, local copies, waits for them, and re-layouts  6.55 us
  transfers between devices with their start and end apart: 20, of which 8 were waited for; matrix products, arithmetic and copies ran while one was open for 3% of the time, Pallas kernels for 34%

profile of v2, /device:TPU:25, one launch (start us, length us, event | category | flops | bytes accessed | tf_op | source)
XLA Modules:
  0.0 151.8 jit_solution(2253506497743641883)
XLA Ops:
  0.6 0.8 pad_add_fusion.facts
  1.4 0.8 copy-done.2
  2.2 0.7 shard_map.149.refs_0_.refs_4_
  3.2 3.1 %collective-permute-start = (bf16[4,2048]{1,0:T(4,128)(2,1)S(1)}, bf16[4,2048]{1,0:T(4,128)(2,1)S(1)}, u32[]{:S(2)}, u32[]{:S(2)}) collective-permute-start(bf16[4,2048]{1,0:T(4,128)(2,1)S(1)} %shard_map.149.refs_0_.refs_4_), channel_id=1, source_target_pairs={{0,1},{1,2},{2,3},{3,0},{4,5},{5,6},{6,7},{7,4},{8,9},{9,10},{10,1... | collective-permute-start | bytes 49160 | tf_op jit(solution)/shard_map/ppermute | solution.py:426
  6.3 1.1 collective-permute-done.2.refs_3_
  7.4 0.6 collective-permute-done.refs_1_
  8.0 1.0 copy-done
  9.0 1.0 copy-done.1
  10.1 2.6 %shard_map.150 = (bf16[64,256]{1,0:T(8,128)(2,1)S(1)}, bf16[64,256]{1,0:T(8,128)(2,1)S(1)}, bf16[64,256]{1,0:T(8,128)(2,1)S(1)}, bf16[64,256]{1,0:T(8,128)(2,1)S(1)}) custom-call(s32[34]{0:T(128)S(1)} %pad_add_fusion.facts, bf16[4,2048]{1,0:T(4,128)(2,1)S(1)} %shard_map.149.refs_0_.refs_4_, bf16[4,2048]{1,0:T(4,128)(2,1)S(1)} %collective-permute-done.refs_1_, ...), custom_call_target="tpu_custom_call" | custom-call | flops 33554432 | bytes 1245184 | tf_op jit(solution)/shard_map/pallas_call | solution.py:407
  12.6 1.3 collective-permute-start.4
  14.0 1.7 %collective-permute-start.5 = (bf16[64,256]{1,0:T(8,128)(2,1)S(1)}, bf16[64,256]{1,0:T(8,128)(2,1)S(1)}, u32[]{:S(2)}, u32[]{:S(2)}) collective-permute-start(bf16[64,256]{1,0:T(8,128)(2,1)S(1)} %get-tuple-element.23), channel_id=1, source_target_pairs={{0,2},{1,3},{2,0},{3,1},{4,6},{5,7},{6,4},{7,5},{8,10},{9,11},{10,... | collective-permute-start | bytes 98312 | tf_op jit(solution)/shard_map/ppermute | solution.py:426
  15.6 0.5 collective-permute-start.6
  16.1 0.9 select_reduce_fusion
  17.1 1.3 collective-permute-start.3
  18.4 1.3 collective-permute-start.11
  19.7 0.7 multiply_add_fusion
  20.4 0.7 copy-done.4
  21.1 0.7 copy-done.5
  21.8 1.6 %shard_map.151 = bf16[8,4,2048]{2,1,0:T(4,128)(2,1)} custom-call(s32[34]{0:T(128)S(1)} %pad_add_fusion.facts, bf16[64,256]{1,0:T(8,128)(2,1)S(1)} %get-tuple-element.21.refs_0_, bf16[64,256]{1,0:T(8,128)(2,1)S(1)} %collective-permute-done.4.refs_1_, bf16[64,256]{1,0:T(8,128)(2,1)S(1)} %collective-permute-done.5.refs_2_, ...), custom_call_target="tpu_custom_call" | custom-call | flops 262144 | bytes 294912 | tf_op jit(solution)/shard_map/pallas_call | solution.py:407
  23.4 7.5 %all-to-all-start = ((bf16[8,4,2048]{2,1,0:T(4,128)(2,1)}), bf16[8,4,2048]{2,1,0:T(4,128)(2,1)S(1)}, u32[]{:S(2)}, u32[]{:S(2)}) async-start(bf16[8,4,2048]{2,1,0:T(4,128)(2,1)} %shard_map.151), calls=%async_computation | async-start | bytes 262144 | tf_op jit(solution)/shard_map/all_to_all | solution.py:464
  30.9 0.7 fusion.1.pick_ref
  31.6 4.0 %all-to-all-done.parts_ref = bf16[8,4,2048]{2,1,0:T(4,128)(2,1)S(1)} async-done(((bf16[8,4,2048]{2,1,0:T(4,128)(2,1)}), bf16[8,4,2048]{2,1,0:T(4,128)(2,1)S(1)}, u32[]{:S(2)}, u32[]{:S(2)}) %all-to-all-start) | async-done | bytes 131104 | tf_op jit(solution)/shard_map/all_to_all | solution.py:464
  35.6 0.7 copy-done.6
  36.2 4.1 %shard_map.152.refs_0_ = bf16[16,1024]{1,0:T(8,128)(2,1)} custom-call(bf16[16,32]{1,0:T(8,128)(2,1)} %fusion.1.pick_ref, bf16[8,4,2048]{2,1,0:T(4,128)(2,1)} %copy-done.6, bf16[2048,1024]{1,0:T(8,128)(2,1)} %weight_ref.2), custom_call_target="tpu_custom_call" | custom-call | flops 67108864 | bytes 4359168 | tf_op jit(solution)/shard_map/pallas_call | solution.py:407
  40.3 2.4 %collective-permute-start.9 = (bf16[16,1024]{1,0:T(8,128)(2,1)}, bf16[16,1024]{1,0:T(8,128)(2,1)S(1)}, u32[]{:S(2)}, u32[]{:S(2)}) collective-permute-start(bf16[16,1024]{1,0:T(8,128)(2,1)} %shard_map.152.refs_0_), channel_id=1, source_target_pairs={{0,3},{1,0},{2,1},{3,2},{4,7},{5,4},{6,5},{7,6},{8,11},{9,8},{10,9... | collective-permute-start | bytes 98312 | tf_op jit(solution)/shard_map/ppermute | solution.py:426
  42.7 2.2 %collective-permute-start.8 = (bf16[16,1024]{1,0:T(8,128)(2,1)}, bf16[16,1024]{1,0:T(8,128)(2,1)S(1)}, u32[]{:S(2)}, u32[]{:S(2)}) collective-permute-start(bf16[16,1024]{1,0:T(8,128)(2,1)} %shard_map.152.refs_0_), channel_id=1, source_target_pairs={{0,2},{1,3},{2,0},{3,1},{4,6},{5,7},{6,4},{7,5},{8,10},{9,11},{10,... | collective-permute-start | bytes 98312 | tf_op jit(solution)/shard_map/ppermute | solution.py:426
  44.9 1.2 collective-permute-start.7
  46.1 0.6 reshape.10.refs_5_
  46.7 1.4 collective-permute-done.7.refs_1_
  48.2 0.6 copy-done.9
  48.8 9.7 %shard_map.154 = (f32[16,1024]{1,0:T(8,128)}, bf16[8,16,1152]{2,1,0:T(8,128)(2,1)}) custom-call(bf16[16,1024]{1,0:T(8,128)(2,1)} %shard_map.152.refs_0_, bf16[16,1024]{1,0:T(8,128)(2,1)} %copy-done.9, bf16[16,1024]{1,0:T(8,128)(2,1)} %copy-done.8, bf16[16,1024]{1,0:T(8,128)(2,1)} %copy-done.7, bf16[16,1024]{1,0:T(8,128)(2,1)} %refs_4_.5, ...), custom_call_target="tpu_custom_call" | custom-call | flops 268435456 | bytes 17303552 | tf_op jit(solution)/shard_map/pallas_call | solution.py:407
  58.5 5.6 %all-to-all-start.1 = ((bf16[8,16,1152]{2,1,0:T(8,128)(2,1)}), bf16[8,16,1152]{2,1,0:T(8,128)(2,1)S(1)}, u32[]{:S(2)}, u32[]{:S(2)}) async-start(bf16[8,16,1152]{2,1,0:T(8,128)(2,1)} %get-tuple-element.30), calls=%async_computation.1 | async-start | bytes 589824 | tf_op jit(solution)/shard_map/all_to_all | solution.py:464
  64.1 1.3 collective-permute-start.10
  65.4 1.3 collective-permute-start.12
  66.7 3.2 %all-to-all-done.1.parts_ref = bf16[8,16,1152]{2,1,0:T(8,128)(2,1)S(1)} async-done(((bf16[8,16,1152]{2,1,0:T(8,128)(2,1)}), bf16[8,16,1152]{2,1,0:T(8,128)(2,1)S(1)}, u32[]{:S(2)}, u32[]{:S(2)}) %all-to-all-start.1) | async-done | bytes 294944 | tf_op jit(solution)/shard_map/all_to_all | solution.py:464
  70.1 9.2 %all_to_all.15.parts_ref = bf16[8,16,512]{2,1,0:T(8,128)(2,1)} all-to-all(bf16[8,16,512]{2,1,0:T(8,128)(2,1)S(1)} %shard_map.155), channel_id=1, replica_groups=mesh['grp'=8,'seq'=4] {'grp'}, dimensions={0} | all-to-all | bytes 262144 | tf_op jit(solution)/shard_map/all_to_all | solution.py:464
  79.3 7.8 %shard_map.156 = (f32[16,256]{1,0:T(8,128)}, f32[16,256]{1,0:T(8,128)}, f32[16,256]{1,0:T(8,128)}, f32[16,256]{1,0:T(8,128)}) custom-call(s32[34]{0:T(128)} %copy-done.3, bf16[8,16,512]{2,1,0:T(8,128)(2,1)} %all_to_all.15.parts_ref, bf16[4096,1024]{1,0:T(8,128)(2,1)} %weight_ref.3), custom_call_target="tpu_custom_call" | custom-call | flops 134217728 | bytes 8585216 | tf_op jit(solution)/shard_map/pallas_call | solution.py:407
  87.1 3.1 %collective-permute-start.13 = (f32[16,256]{1,0:T(8,128)}, f32[16,256]{1,0:T(8,128)S(1)}, u32[]{:S(2)}, u32[]{:S(2)}) collective-permute-start(f32[16,256]{1,0:T(8,128)} %get-tuple-element.31), channel_id=1, source_target_pairs={{0,1},{1,2},{2,3},{3,0},{4,5},{5,6},{6,7},{7,4},{8,9},{9,10},{10,1... | collective-permute-start | bytes 49160 | tf_op jit(solution)/shard_map/ppermute | solution.py:426
  90.2 0.4 collective-permute-start.15
  90.6 0.7 collective-permute-done.13
  91.3 2.6 %collective-permute-done.14 = f32[16,256]{1,0:T(8,128)S(1)} collective-permute-done((f32[16,256]{1,0:T(8,128)}, f32[16,256]{1,0:T(8,128)S(1)}, u32[]{:S(2)}, u32[]{:S(2)}) %collective-permute-start.14) | collective-permute-done | bytes 16416 | tf_op jit(solution)/shard_map/ppermute | solution.py:426
  93.9 0.9 collective-permute-done.15
  94.8 1.3 add_convert_fusion
  96.1 1.3 collective-permute-start.16
  97.4 1.5 collective-permute-start.17
  98.9 27.7 %shard_map.153 = (bf16[256,8192]{1,0:T(8,128)(2,1)}, f32[8,256,8]{2,1,0:T(8,128)}) custom-call(s32[34]{0:T(128)} %copy-done.3, bf16[256,8192]{1,0:T(8,128)(2,1)} %query_ref.3, bf16[256,1024]{1,0:T(8,128)(2,1)} %refs_1_.1, bf16[256,1024]{1,0:T(8,128)(2,1)} %copy-done.11, bf16[256,1024]{1,0:T(8,128)(2,1)} %copy-done.13, bf16[256,1024]{1,0:T(8,128)(2,1)} %refs_4_.4, ...), custom_call_target="tpu_custom_call" | custom-call | flops 12884901888 | bytes 11599872 | tf_op jit(solution)/shard_map/pallas_call | solution.py:407
  126.7 0.8 copy-done.15
  127.6 24.2 %shard_map.157 = bf16[256,8192]{1,0:T(8,128)(2,1)} custom-call(s32[34]{0:T(128)} %copy-done.3, bf16[256,8192]{1,0:T(8,128)(2,1)} %get-tuple-element.28.near_ref, f32[8,256,8]{2,1,0:T(8,128)} %get-tuple-element.29.level_ref, bf16[256,8192]{1,0:T(8,128)(2,1)} %query_ref.3, bf16[256,1024]{1,0:T(8,128)(2,1)} %copy-done.15, ...), custom_call_target="tpu_custom_call", output_to_operand_aliasing={{}: (1, {})} | custom-call | flops 4294967296 | bytes 13697024 | tf_op jit(solution)/shard_map/pallas_call | solution.py:407
  (42 shorter events, 0.7 us)
Async XLA Ops:
  0.6 45.5 %copy-start.10 = (bf16[1024]{0:T(1024)(128)(2,1)S(1)}, bf16[1024]{0:T(1024)(128)(2,1)}, u32[]{:S(2)}) copy-start(bf16[1024]{0:T(1024)(128)(2,1)} %param.24) | copy-start | bytes 6148
  1.4 0.8 copy-start.2
  2.2 56.2 %copy-start.3 = (s32[34]{0:T(128)}, s32[34]{0:T(128)S(1)}, u32[]{:S(2)}) copy-start(s32[34]{0:T(128)S(1)} %pad_add_fusion.facts) | copy-start | bytes 412
  3.0 4.4 %collective-permute-start.2 = (bf16[4,2048]{1,0:T(4,128)(2,1)S(1)}, bf16[4,2048]{1,0:T(4,128)(2,1)S(1)}, u32[]{:S(2)}, u32[]{:S(2)}) collective-permute-start(bf16[4,2048]{1,0:T(4,128)(2,1)S(1)} %shard_map.149.refs_0_.refs_4_), channel_id=1, source_target_pairs={{0,3},{1,0},{2,1},{3,2},{4,7},{5,4},{6,5},{7,6},{8,11},{9,8},{10,9... | collective-permute-start | bytes 49160 | tf_op jit(solution)/shard_map/ppermute | solution.py:426
  3.2 4.2 %collective-permute-start.1 = (bf16[4,2048]{1,0:T(4,128)(2,1)S(1)}, bf16[4,2048]{1,0:T(4,128)(2,1)S(1)}, u32[]{:S(2)}, u32[]{:S(2)}) collective-permute-start(bf16[4,2048]{1,0:T(4,128)(2,1)S(1)} %shard_map.149.refs_0_.refs_4_), channel_id=1, source_target_pairs={{0,2},{1,3},{2,0},{3,1},{4,6},{5,7},{6,4},{7,5},{8,10},{9,11},{10,... | collective-permute-start | bytes 49160 | tf_op jit(solution)/shard_map/ppermute | solution.py:426
  3.2 4.8 %collective-permute-start = (bf16[4,2048]{1,0:T(4,128)(2,1)S(1)}, bf16[4,2048]{1,0:T(4,128)(2,1)S(1)}, u32[]{:S(2)}, u32[]{:S(2)}) collective-permute-start(bf16[4,2048]{1,0:T(4,128)(2,1)S(1)} %shard_map.149.refs_0_.refs_4_), channel_id=1, source_target_pairs={{0,1},{1,2},{2,3},{3,0},{4,5},{5,6},{6,7},{7,4},{8,9},{9,10},{10,1... | collective-permute-start | bytes 49160 | tf_op jit(solution)/shard_map/ppermute | solution.py:426
  8.0 1.0 copy-start
  9.0 1.0 copy-start.1
  12.6 5.7 %collective-permute-start.4 = (bf16[64,256]{1,0:T(8,128)(2,1)S(1)}, bf16[64,256]{1,0:T(8,128)(2,1)S(1)}, u32[]{:S(2)}, u32[]{:S(2)}) collective-permute-start(bf16[64,256]{1,0:T(8,128)(2,1)S(1)} %get-tuple-element.22), channel_id=1, source_target_pairs={{0,3},{1,0},{2,1},{3,2},{4,7},{5,4},{6,5},{7,6},{8,11},{9,8},{10,9... | collective-permute-start | bytes 98312 | tf_op jit(solution)/shard_map/ppermute | solution.py:426
  14.0 4.4 %collective-permute-start.5 = (bf16[64,256]{1,0:T(8,128)(2,1)S(1)}, bf16[64,256]{1,0:T(8,128)(2,1)S(1)}, u32[]{:S(2)}, u32[]{:S(2)}) collective-permute-start(bf16[64,256]{1,0:T(8,128)(2,1)S(1)} %get-tuple-element.23), channel_id=1, source_target_pairs={{0,2},{1,3},{2,0},{3,1},{4,6},{5,7},{6,4},{7,5},{8,10},{9,11},{10,... | collective-permute-start | bytes 98312 | tf_op jit(solution)/shard_map/ppermute | solution.py:426
  15.6 2.8 %collective-permute-start.6 = (bf16[64,256]{1,0:T(8,128)(2,1)S(1)}, bf16[64,256]{1,0:T(8,128)(2,1)S(1)}, u32[]{:S(2)}, u32[]{:S(2)}) collective-permute-start(bf16[64,256]{1,0:T(8,128)(2,1)S(1)} %get-tuple-element.24), channel_id=1, source_target_pairs={{0,1},{1,2},{2,3},{3,0},{4,5},{5,6},{6,7},{7,4},{8,9},{9,10},{10,1... | collective-permute-start | bytes 98312 | tf_op jit(solution)/shard_map/ppermute | solution.py:426
  17.1 47.0 %collective-permute-start.3 = (bf16[256,1024]{1,0:T(8,128)(2,1)}, bf16[256,1024]{1,0:T(8,128)(2,1)S(1)}, u32[]{:S(2)}, u32[]{:S(2)}) collective-permute-start(bf16[256,1024]{1,0:T(8,128)(2,1)} %refs_1_.1), channel_id=1, source_target_pairs={{0,1},{1,2},{2,3},{4,5},{5,6},{6,7},{8,9},{9,10},{10,11},{12,13},{... | collective-permute-start | bytes 1572872 | tf_op jit(solution)/shard_map/ppermute | solution.py:468
  18.4 47.0 %collective-permute-start.11 = (bf16[256,1024]{1,0:T(8,128)(2,1)}, bf16[256,1024]{1,0:T(8,128)(2,1)S(1)}, u32[]{:S(2)}, u32[]{:S(2)}) collective-permute-start(bf16[256,1024]{1,0:T(8,128)(2,1)} %refs_4_.4), channel_id=1, source_target_pairs={{0,1},{1,2},{2,3},{4,5},{5,6},{6,7},{8,9},{9,10},{10,11},{12,13},{... | collective-permute-start | bytes 1572872 | tf_op jit(solution)/shard_map/ppermute | solution.py:468
  20.4 0.7 copy-start.4
  21.1 0.7 copy-start.5
  23.4 12.2 %all-to-all-start = ((bf16[8,4,2048]{2,1,0:T(4,128)(2,1)}), bf16[8,4,2048]{2,1,0:T(4,128)(2,1)S(1)}, u32[]{:S(2)}, u32[]{:S(2)}) async-start(bf16[8,4,2048]{2,1,0:T(4,128)(2,1)} %shard_map.151), calls=%async_computation | async-start | bytes 262144 | tf_op jit(solution)/shard_map/all_to_all | solution.py:464
  35.6 0.7 copy-start.6
  40.3 6.4 %collective-permute-start.9 = (bf16[16,1024]{1,0:T(8,128)(2,1)}, bf16[16,1024]{1,0:T(8,128)(2,1)S(1)}, u32[]{:S(2)}, u32[]{:S(2)}) collective-permute-start(bf16[16,1024]{1,0:T(8,128)(2,1)} %shard_map.152.refs_0_), channel_id=1, source_target_pairs={{0,3},{1,0},{2,1},{3,2},{4,7},{5,4},{6,5},{7,6},{8,11},{9,8},{10,9... | collective-permute-start | bytes 98312 | tf_op jit(solution)/shard_map/ppermute | solution.py:426
  42.7 4.0 %collective-permute-start.8 = (bf16[16,1024]{1,0:T(8,128)(2,1)}, bf16[16,1024]{1,0:T(8,128)(2,1)S(1)}, u32[]{:S(2)}, u32[]{:S(2)}) collective-permute-start(bf16[16,1024]{1,0:T(8,128)(2,1)} %shard_map.152.refs_0_), channel_id=1, source_target_pairs={{0,2},{1,3},{2,0},{3,1},{4,6},{5,7},{6,4},{7,5},{8,10},{9,11},{10,... | collective-permute-start | bytes 98312 | tf_op jit(solution)/shard_map/ppermute | solution.py:426
  44.9 3.3 %collective-permute-start.7 = (bf16[16,1024]{1,0:T(8,128)(2,1)}, bf16[16,1024]{1,0:T(8,128)(2,1)S(1)}, u32[]{:S(2)}, u32[]{:S(2)}) collective-permute-start(bf16[16,1024]{1,0:T(8,128)(2,1)} %shard_map.152.refs_0_), channel_id=1, source_target_pairs={{0,1},{1,2},{2,3},{3,0},{4,5},{5,6},{6,7},{7,4},{8,9},{9,10},{10,1... | collective-permute-start | bytes 98312 | tf_op jit(solution)/shard_map/ppermute | solution.py:426
  46.7 1.5 copy-start.7
  46.7 1.5 copy-start.8
  48.2 0.6 copy-start.9
  58.5 11.4 %all-to-all-start.1 = ((bf16[8,16,1152]{2,1,0:T(8,128)(2,1)}), bf16[8,16,1152]{2,1,0:T(8,128)(2,1)S(1)}, u32[]{:S(2)}, u32[]{:S(2)}) async-start(bf16[8,16,1152]{2,1,0:T(8,128)(2,1)} %get-tuple-element.30), calls=%async_computation.1 | async-start | bytes 589824 | tf_op jit(solution)/shard_map/all_to_all | solution.py:464
  64.1 23.0 %copy-start.11 = (bf16[256,1024]{1,0:T(8,128)(2,1)}, bf16[256,1024]{1,0:T(8,128)(2,1)S(1)}, u32[]{:S(2)}) copy-start(bf16[256,1024]{1,0:T(8,128)(2,1)S(1)} %collective-permute-done.3.refs_2_) | copy-start | bytes 1572868
  64.1 32.1 %collective-permute-start.10 = (bf16[256,1024]{1,0:T(8,128)(2,1)S(1)}, bf16[256,1024]{1,0:T(8,128)(2,1)S(1)}, u32[]{:S(2)}, u32[]{:S(2)}) collective-permute-start(bf16[256,1024]{1,0:T(8,128)(2,1)S(1)} %collective-permute-done.3.refs_2_), channel_id=1, source_target_pairs={{1,2},{2,3},{5,6},{6,7},{9,10},{10,11},{13,14},{14,15},{17,18},{18... | collective-permute-start | bytes 1572872 | tf_op jit(solution)/shard_map/ppermute | solution.py:468
  65.4 21.7 %copy-start.12 = (bf16[256,1024]{1,0:T(8,128)(2,1)}, bf16[256,1024]{1,0:T(8,128)(2,1)S(1)}, u32[]{:S(2)}) copy-start(bf16[256,1024]{1,0:T(8,128)(2,1)S(1)} %collective-permute-done.11.refs_5_) | copy-start | bytes 1572868
  65.4 32.0 %collective-permute-start.12 = (bf16[256,1024]{1,0:T(8,128)(2,1)S(1)}, bf16[256,1024]{1,0:T(8,128)(2,1)S(1)}, u32[]{:S(2)}, u32[]{:S(2)}) collective-permute-start(bf16[256,1024]{1,0:T(8,128)(2,1)S(1)} %collective-permute-done.11.refs_5_), channel_id=1, source_target_pairs={{1,2},{2,3},{5,6},{6,7},{9,10},{10,11},{13,14},{14,15},{17,18},{18... | collective-permute-start | bytes 1572872 | tf_op jit(solution)/shard_map/ppermute | solution.py:468
  87.1 4.2 %collective-permute-start.13 = (f32[16,256]{1,0:T(8,128)}, f32[16,256]{1,0:T(8,128)S(1)}, u32[]{:S(2)}, u32[]{:S(2)}) collective-permute-start(f32[16,256]{1,0:T(8,128)} %get-tuple-element.31), channel_id=1, source_target_pairs={{0,1},{1,2},{2,3},{3,0},{4,5},{5,6},{6,7},{7,4},{8,9},{9,10},{10,1... | collective-permute-start | bytes 49160 | tf_op jit(solution)/shard_map/ppermute | solution.py:426
  90.2 3.7 %collective-permute-start.14 = (f32[16,256]{1,0:T(8,128)}, f32[16,256]{1,0:T(8,128)S(1)}, u32[]{:S(2)}, u32[]{:S(2)}) collective-permute-start(f32[16,256]{1,0:T(8,128)} %get-tuple-element.32), channel_id=1, source_target_pairs={{0,2},{1,3},{2,0},{3,1},{4,6},{5,7},{6,4},{7,5},{8,10},{9,11},{10,... | collective-permute-start | bytes 49160 | tf_op jit(solution)/shard_map/ppermute | solution.py:426
  90.2 4.6 %collective-permute-start.15 = (f32[16,256]{1,0:T(8,128)}, f32[16,256]{1,0:T(8,128)S(1)}, u32[]{:S(2)}, u32[]{:S(2)}) collective-permute-start(f32[16,256]{1,0:T(8,128)} %get-tuple-element.33), channel_id=1, source_target_pairs={{0,3},{1,0},{2,1},{3,2},{4,7},{5,4},{6,5},{7,6},{8,11},{9,8},{10,9... | collective-permute-start | bytes 49160 | tf_op jit(solution)/shard_map/ppermute | solution.py:426
  96.1 2.8 %copy-start.13 = (bf16[256,1024]{1,0:T(8,128)(2,1)}, bf16[256,1024]{1,0:T(8,128)(2,1)S(1)}, u32[]{:S(2)}) copy-start(bf16[256,1024]{1,0:T(8,128)(2,1)S(1)} %collective-permute-done.10.refs_3_) | copy-start | bytes 1572868
  96.1 30.5 %collective-permute-start.16 = (bf16[256,1024]{1,0:T(8,128)(2,1)S(1)}, bf16[256,1024]{1,0:T(8,128)(2,1)S(1)}, u32[]{:S(2)}, u32[]{:S(2)}) collective-permute-start(bf16[256,1024]{1,0:T(8,128)(2,1)S(1)} %collective-permute-done.10.refs_3_), channel_id=1, source_target_pairs={{2,3},{6,7},{10,11},{14,15},{18,19},{22,23},{26,27},{30,31}} | collective-permute-start | bytes 1572872 | tf_op jit(solution)/shard_map/ppermute | solution.py:468
  97.4 1.5 copy-start.14
  97.4 29.2 %collective-permute-start.17 = (bf16[256,1024]{1,0:T(8,128)(2,1)S(1)}, bf16[256,1024]{1,0:T(8,128)(2,1)S(1)}, u32[]{:S(2)}, u32[]{:S(2)}) collective-permute-start(bf16[256,1024]{1,0:T(8,128)(2,1)S(1)} %collective-permute-done.12.refs_6_), channel_id=1, source_target_pairs={{2,3},{6,7},{10,11},{14,15},{18,19},{22,23},{26,27},{30,31}} | collective-permute-start | bytes 1572872 | tf_op jit(solution)/shard_map/ppermute | solution.py:468
  126.7 0.8 copy-start.15
  126.7 1.0 copy-start.16
